TPU v7x, 32 devices: a whole 2x2x4 slice. The times are simulated.
32 devices in a mesh: grp: 1, dap: 32 (over z, y, x, core), sub: 1.
Axes of the slice: x: 2, y: 2, z: 4, core: 2. Of those that a mesh axis runs over, the one named last changes fastest.
Arguments:
- homolog_embedding: bfloat16 [32, 128, 256], P(('grp', 'sub'), 'dap'), may hold values from -6 to 6
- alignment_mask: int32 [32, 128], P(('grp', 'sub'), 'dap'), may hold values from 0 to 1, as said below
- pair_activation: bfloat16 [128, 128, 128], P(('grp', 'dap'), 'sub'), may hold values from -6 to 6
- sequence_mask: int32 [128], P('grp'), may hold values from 0 to 1, as said below
- homolog_scaling_factor: float32 [256], replicated, may hold values from 0.1 to 1.9
- homolog_mapping_matrix: bfloat16 [256, 64], replicated, may hold values from -0.375 to 0.375
- outer_output_weight: bfloat16 [1024, 128], replicated, may hold values from -0.5 to 0.5
- outer_output_bias: float32 [128], replicated, may hold values from -3 to 3
- pair_norm_gains: float32 [4, 128], replicated, may hold values from 0.1 to 1.9
- triangle_input_weights: bfloat16 [2, 128, 640], replicated, may hold values from -0.5 to 0.5
- triangle_output_weights: bfloat16 [2, 128, 128], replicated, may hold values from -0.5 to 0.5
Outputs:
- pair_out: bfloat16 [128, 128, 128], P(('grp', 'dap'), 'sub')
Inputs may be any that keep to these rules, and one draw needn't show every extreme that they name: `sequence_mask`: 1 on the first residues of the crop and 0 on the rest; between 1 and 32 residues are padding. `alignment_mask`: 0 wherever sequence_mask is 0.
All inputs are finite; a program needn't handle non-finite values.
Results may differ from a plain program's by a relative error of at most 0.017.
Values may be sent and summed in bfloat16 or wider, within the bound.
A program may use at most 64 MiB of HBM per device.

v0:
```python
import jax
import jax.numpy as jnp
from jax import lax
from jax.sharding import PartitionSpec as P


def apply_layer_norm(values, norm_gain, dimension):
    center = values - jnp.mean(values, dimension, keepdims=True)
    spread = jnp.mean(center * center, dimension, keepdims=True)
    return center * lax.rsqrt(spread + 1e-05) * norm_gain


def triangle(current, pair_mask, norm_in, norm_out, weight_in, weight_out, outgoing):
    width = weight_out.shape[0]
    normed = apply_layer_norm(current.astype(jnp.float32), norm_in, 2).astype(jnp.bfloat16)
    projected_alignment = jnp.einsum(
        "rhk,kc->crh", normed, weight_in, preferred_element_type=jnp.float32
    )
    left_value = projected_alignment[:width]
    right_value = projected_alignment[width : 2 * width]
    left_gate = projected_alignment[2 * width : 3 * width]
    right_gate = projected_alignment[3 * width : 4 * width]
    gating = jax.nn.sigmoid(projected_alignment[4 * width :])
    left_side = (pair_mask[None] * jax.nn.sigmoid(left_gate) * left_value).astype(jnp.bfloat16)
    right_side = (pair_mask[None] * jax.nn.sigmoid(right_gate) * right_value).astype(jnp.bfloat16)
    left_channels, right_channels = (
        lax.all_to_all(left_side, "dap", split_axis=0, concat_axis=1, tiled=True),
        lax.all_to_all(right_side, "dap", split_axis=0, concat_axis=1, tiled=True),
    )
    if outgoing:
        left_full = lax.all_gather(left_channels, "sub", axis=2, tiled=True)
        right_rows = lax.all_to_all(right_channels, "sub", split_axis=1, concat_axis=2, tiled=True)
        mixed = jnp.einsum(
            "cik,cjk->cij", left_full, right_rows, preferred_element_type=jnp.float32
        )
    else:
        left_full = lax.all_gather(left_channels, "sub", axis=2, tiled=True)
        mixed = jnp.einsum(
            "cki,ckj->cij", left_full, right_channels, preferred_element_type=jnp.float32
        )
    returned = lax.all_to_all(
        mixed.astype(jnp.bfloat16), "dap", split_axis=1, concat_axis=0, tiled=True
    )
    mixed_norm = apply_layer_norm(returned.astype(jnp.float32), norm_out[:, None, None], 0).astype(
        jnp.bfloat16
    )
    update = jnp.einsum("crh,cd->drh", mixed_norm, weight_out, preferred_element_type=jnp.float32)
    return (current.astype(jnp.float32) + jnp.transpose(gating * update, (1, 2, 0))).astype(
        jnp.bfloat16
    )


def local(
    homolog_embedding,
    alignment_mask,
    pair_activation,
    sequence_mask,
    homolog_scaling_factor,
    homolog_mapping_matrix,
    outer_output_weight,
    outer_output_bias,
    pair_norm_gains,
    triangle_input_weights,
    triangle_output_weights,
):
    outer_product_width = homolog_mapping_matrix.shape[1] // 2
    alignment_row_count = pair_activation.shape[0]
    column_halfway = pair_activation.shape[1]
    row_halfway = homolog_embedding.shape[0]
    dap_index = lax.axis_index("dap")
    sub_index = lax.axis_index("sub")
    alignment_normed = apply_layer_norm(
        homolog_embedding.astype(jnp.float32), homolog_scaling_factor, 2
    ).astype(jnp.bfloat16)
    mask_as_float = alignment_mask.astype(jnp.float32)
    projected_alignment = (
        jnp.einsum(
            "ftv,vy->fty",
            alignment_normed,
            homolog_mapping_matrix,
            preferred_element_type=jnp.float32,
        )
        * mask_as_float[:, :, None]
    )
    left_proj = (
        projected_alignment[:, :, :outer_product_width]
        .astype(jnp.bfloat16)
        .reshape(row_halfway, alignment_row_count * outer_product_width)
    )
    right_proj = (
        projected_alignment[:, :, outer_product_width:]
        .astype(jnp.bfloat16)
        .reshape(row_halfway, alignment_row_count * outer_product_width)
    )
    mask_bits = mask_as_float.astype(jnp.bfloat16)
    left_complete, right_all, mask_all = (
        lax.all_gather(left_proj, "sub", axis=0, tiled=True),
        lax.all_gather(right_proj, "sub", axis=0, tiled=True),
        lax.all_gather(mask_bits, "sub", axis=0, tiled=True),
    )
    right_wide, mask_wide = (
        lax.all_gather(right_all, "dap", axis=1, tiled=True),
        lax.all_gather(mask_all, "dap", axis=1, tiled=True),
    )
    right_column_block = lax.dynamic_slice_in_dim(
        right_wide,
        sub_index * (column_halfway * outer_product_width),
        column_halfway * outer_product_width,
        1,
    )
    mask_cols = lax.dynamic_slice_in_dim(mask_wide, sub_index * column_halfway, column_halfway, 1)
    alignment_mask_total = left_complete.shape[0]
    left_row_block = jnp.transpose(
        left_complete.reshape(alignment_mask_total, alignment_row_count, outer_product_width),
        (1, 0, 2),
    )
    right_value_grid = right_column_block.reshape(
        alignment_mask_total, column_halfway, outer_product_width
    )
    counts = jnp.dot(mask_all.T, mask_cols, preferred_element_type=jnp.float32)

    def opm_row(packed):
        left_row, count_row, pair_row = packed
        outer_prod = jnp.einsum(
            "sp,shq->hpq", left_row, right_value_grid, preferred_element_type=jnp.float32
        )
        outer_prod = outer_prod.astype(jnp.bfloat16).reshape(
            column_halfway, outer_product_width * outer_product_width
        )
        values = (
            jnp.dot(outer_prod, outer_output_weight, preferred_element_type=jnp.float32)
            + outer_output_bias
        )
        return (
            pair_row.astype(jnp.float32) + values / jnp.maximum(count_row, 1.0)[:, None]
        ).astype(jnp.bfloat16)

    current = lax.map(opm_row, (left_row_block, counts, pair_activation))
    seq_float = sequence_mask.astype(jnp.float32)
    row_mask = lax.dynamic_slice_in_dim(
        seq_float, dap_index * alignment_row_count, alignment_row_count
    )
    col_mask = lax.dynamic_slice_in_dim(seq_float, sub_index * column_halfway, column_halfway)
    pair_mask = row_mask[:, None] * col_mask[None, :]
    for which in range(2):
        current = triangle(
            current,
            pair_mask,
            pair_norm_gains[2 * which],
            pair_norm_gains[2 * which + 1],
            triangle_input_weights[which],
            triangle_output_weights[which],
            which == 0,
        )
    return current


def solution(mesh):
    return jax.shard_map(
        local,
        mesh=mesh,
        in_specs=(
            P(("grp", "sub"), "dap", None),
            P(("grp", "sub"), "dap"),
            P(("grp", "dap"), "sub", None),
            P("grp"),
            P(),
            P(),
            P(),
            P(),
            P(),
            P(),
            P(),
        ),
        out_specs=P(("grp", "dap"), "sub", None),
        check_vma=False,
    )
```

profile of v0, /device:TPU:0, one launch (start us, length us, event | category | flops | bytes accessed | tf_op | source)
XLA Modules:
  0.0 164.7 jit_solution(7375411504323518462)
XLA Ops:
  0.0 1.0 convert_reduce_fusion.1
  1.0 1.0 fusion.65
  2.7 1.0 fusion.67
  4.1 43.9 %all_gather.4 = bf16[32,4096]{1,0:T(8,128)(2,1)S(1)} all-gather(bf16[32,128]{1,0:T(8,128)(2,1)S(1)} %reshape.125), channel_id=1, replica_groups=mesh['grp'=1,'dap'=32,'sub'=1] {'dap'}, dimensions={1}, use_global_device_ids=true | all-gather | bytes 270336 | tf_op jit(solution)/shard_map/all_gather | solution.py:102
  48.0 0.8 reshape.126
  49.3 36.7 %all-gather = bf16[32,4,32]{2,1,0:T(4,128)(2,1)S(1)} all-gather(bf16[1,4,32]{2,1,0:T(4,128)(2,1)S(1)} %get-tuple-element.100), channel_id=1, replica_groups=mesh['grp'=1,'dap'=32,'sub'=1] {'dap'}, dimensions={0}, use_global_device_ids=true | all-gather | bytes 8448 | tf_op jit(solution)/shard_map/all_gather | solution.py:103
  86.2 5.8 %while.10 = (s32[]{:T(128)}, bf16[4,128,128]{2,1,0:T(8,128)(2,1)S(1)}, bf16[4,128,128]{2,1,0:T(8,128)(2,1)}, bf16[4,32,32]{2,1,0:T(8,128)(2,1)S(1)}, bf16[32,128...) while((s32[]{:T(128)}, ...), condition=%wide.region_3.4_spmd, body=%wide.region_2.3_spmd.sunk | while | flops 42156160 | bytes 1648745 | solution.py:138
  86.6 1.0 fusion.109
  88.0 1.0 fusion.109
  89.5 1.0 fusion.109
  91.0 1.0 fusion.109
  94.0 2.6 %all-to-all-start = ((bf16[128,4,128]{2,1,0:T(4,128)(2,1)}), bf16[128,4,128]{2,1,0:T(4,128)(2,1)S(1)}, u32[]{:S(2)}, u32[]{:S(2)}) async-start(bf16[128,4,128]{2,1,0:T(4,128)(2,1)} %copy.49), calls=%async_computation | async-start | bytes 262144 | tf_op jit(solution)/shard_map/all_to_all | solution.py:27
  97.3 7.5 %all-to-all-done = bf16[128,4,128]{2,1,0:T(4,128)(2,1)S(1)} async-done(((bf16[128,4,128]{2,1,0:T(4,128)(2,1)}), bf16[128,4,128]{2,1,0:T(4,128)(2,1)S(1)}, u32[]{:S(2)}, u32[]{:S(2)}) %all-to-all-start) | async-done | bytes 131104 | tf_op jit(solution)/shard_map/all_to_all | solution.py:27
  104.8 2.6 %all-to-all-start.1 = ((bf16[128,4,128]{2,1,0:T(4,128)(2,1)}), bf16[128,4,128]{2,1,0:T(4,128)(2,1)S(1)}, u32[]{:S(2)}, u32[]{:S(2)}) async-start(bf16[128,4,128]{2,1,0:T(4,128)(2,1)} %copy.52), calls=%async_computation.1 | async-start | bytes 262144 | tf_op jit(solution)/shard_map/all_to_all | solution.py:28
  107.5 8.1 %all-to-all-done.1 = bf16[128,4,128]{2,1,0:T(4,128)(2,1)S(1)} async-done(((bf16[128,4,128]{2,1,0:T(4,128)(2,1)}), bf16[128,4,128]{2,1,0:T(4,128)(2,1)S(1)}, u32[]{:S(2)}, u32[]{:S(2)}) %all-to-all-start.1) | async-done | bytes 131104 | tf_op jit(solution)/shard_map/all_to_all | solution.py:28
  116.7 2.6 %all-to-all-start.2 = ((bf16[4,128,128]{2,0,1:T(4,128)(2,1)}), bf16[4,128,128]{2,0,1:T(4,128)(2,1)S(1)}, u32[]{:S(2)}, u32[]{:S(2)}) async-start(bf16[4,128,128]{2,0,1:T(4,128)(2,1)} %copy.55), calls=%async_computation.2 | async-start | bytes 262144 | tf_op jit(solution)/shard_map/all_to_all | solution.py:41
  119.4 8.1 %all-to-all-done.2 = bf16[4,128,128]{2,0,1:T(4,128)(2,1)S(1)} async-done(((bf16[4,128,128]{2,0,1:T(4,128)(2,1)}), bf16[4,128,128]{2,0,1:T(4,128)(2,1)S(1)}, u32[]{:S(2)}, u32[]{:S(2)}) %all-to-all-start.2) | async-done | bytes 131104 | tf_op jit(solution)/shard_map/all_to_all | solution.py:41
  129.9 2.6 %all-to-all-start.3 = ((bf16[128,4,128]{2,1,0:T(4,128)(2,1)}), bf16[128,4,128]{2,1,0:T(4,128)(2,1)S(1)}, u32[]{:S(2)}, u32[]{:S(2)}) async-start(bf16[128,4,128]{2,1,0:T(4,128)(2,1)} %copy.59), calls=%async_computation.3 | async-start | bytes 262144 | tf_op jit(solution)/shard_map/all_to_all | solution.py:27
  133.3 7.5 %all-to-all-done.3 = bf16[128,4,128]{2,1,0:T(4,128)(2,1)S(1)} async-done(((bf16[128,4,128]{2,1,0:T(4,128)(2,1)}), bf16[128,4,128]{2,1,0:T(4,128)(2,1)S(1)}, u32[]{:S(2)}, u32[]{:S(2)}) %all-to-all-start.3) | async-done | bytes 131104 | tf_op jit(solution)/shard_map/all_to_all | solution.py:27
  140.7 2.6 %all-to-all-start.4 = ((bf16[128,4,128]{2,1,0:T(4,128)(2,1)}), bf16[128,4,128]{2,1,0:T(4,128)(2,1)S(1)}, u32[]{:S(2)}, u32[]{:S(2)}) async-start(bf16[128,4,128]{2,1,0:T(4,128)(2,1)} %copy.62), calls=%async_computation.4 | async-start | bytes 262144 | tf_op jit(solution)/shard_map/all_to_all | solution.py:28
  143.5 8.1 %all-to-all-done.4 = bf16[128,4,128]{2,1,0:T(4,128)(2,1)S(1)} async-done(((bf16[128,4,128]{2,1,0:T(4,128)(2,1)}), bf16[128,4,128]{2,1,0:T(4,128)(2,1)S(1)}, u32[]{:S(2)}, u32[]{:S(2)}) %all-to-all-start.4) | async-done | bytes 131104 | tf_op jit(solution)/shard_map/all_to_all | solution.py:28
  152.7 2.6 %all-to-all-start.5 = ((bf16[4,128,128]{2,0,1:T(4,128)(2,1)}), bf16[4,128,128]{2,0,1:T(4,128)(2,1)S(1)}, u32[]{:S(2)}, u32[]{:S(2)}) async-start(bf16[4,128,128]{2,0,1:T(4,128)(2,1)} %copy.66), calls=%async_computation.5 | async-start | bytes 262144 | tf_op jit(solution)/shard_map/all_to_all | solution.py:41
  155.4 8.1 %all-to-all-done.5 = bf16[4,128,128]{2,0,1:T(4,128)(2,1)S(1)} async-done(((bf16[4,128,128]{2,0,1:T(4,128)(2,1)}), bf16[4,128,128]{2,0,1:T(4,128)(2,1)S(1)}, u32[]{:S(2)}, u32[]{:S(2)}) %all-to-all-start.5) | async-done | bytes 131104 | tf_op jit(solution)/shard_map/all_to_all | solution.py:41
  163.8 0.9 fusion.19
  (84 shorter events, 12.0 us)
Async XLA Ops:
  0.0 3.7 %copy-start = (bf16[256,64]{0,1:T(8,128)(2,1)S(1)}, bf16[256,64]{0,1:T(8,128)(2,1)}, u32[]{:S(2)}) copy-start(bf16[256,64]{0,1:T(8,128)(2,1)} %param.18) | copy-start | bytes 98308
  48.0 38.0 %copy-start.2 = (s32[32,4]{0,1:T(4,128)S(1)}, s32[32,4]{0,1:T(4,128)}, u32[]{:S(2)}) copy-start(s32[32,4]{0,1:T(4,128)} %param.14) | copy-start | bytes 1540
  48.0 38.2 %copy-start.4 = (bf16[1024,128]{1,0:T(8,128)(2,1)S(1)}, bf16[1024,128]{1,0:T(8,128)(2,1)}, u32[]{:S(2)}) copy-start(bf16[1024,128]{1,0:T(8,128)(2,1)} %param.19) | copy-start | bytes 786436
  48.0 38.2 %copy-start.6 = (f32[128]{0:T(128)S(1)}, f32[128]{0:T(128)}, u32[]{:S(2)}) copy-start(f32[128]{0:T(128)} %param.20) | copy-start | bytes 1540
  86.1 6.3 %copy-start.3 = (f32[4,128]{1,0:T(4,128)S(1)}, f32[4,128]{1,0:T(4,128)}, u32[]{:S(2)}) copy-start(f32[4,128]{1,0:T(4,128)} %param.21) | copy-start | bytes 6148
  86.1 6.3 %copy-start.7 = (s32[128]{0:T(128)S(1)}, s32[128]{0:T(128)}, u32[]{:S(2)}) copy-start(s32[128]{0:T(128)} %param.16) | copy-start | bytes 1540
  86.2 6.4 %copy-start.1 = (bf16[2,128,640]{2,1,0:T(8,128)(2,1)S(1)}, bf16[2,128,640]{2,1,0:T(8,128)(2,1)}, u32[]{:S(2)}) copy-start(bf16[2,128,640]{2,1,0:T(8,128)(2,1)} %param.22) | copy-start | bytes 983044
  94.0 10.8 %all-to-all-start = ((bf16[128,4,128]{2,1,0:T(4,128)(2,1)}), bf16[128,4,128]{2,1,0:T(4,128)(2,1)S(1)}, u32[]{:S(2)}, u32[]{:S(2)}) async-start(bf16[128,4,128]{2,1,0:T(4,128)(2,1)} %copy.49), calls=%async_computation | async-start | bytes 262144 | tf_op jit(solution)/shard_map/all_to_all | solution.py:27
  104.8 10.8 %all-to-all-start.1 = ((bf16[128,4,128]{2,1,0:T(4,128)(2,1)}), bf16[128,4,128]{2,1,0:T(4,128)(2,1)S(1)}, u32[]{:S(2)}, u32[]{:S(2)}) async-start(bf16[128,4,128]{2,1,0:T(4,128)(2,1)} %copy.52), calls=%async_computation.1 | async-start | bytes 262144 | tf_op jit(solution)/shard_map/all_to_all | solution.py:28
  107.4 20.5 %copy-start.5 = (bf16[2,128,128]{2,1,0:T(8,128)(2,1)S(1)}, bf16[2,128,128]{2,1,0:T(8,128)(2,1)}, u32[]{:S(2)}) copy-start(bf16[2,128,128]{2,1,0:T(8,128)(2,1)} %param.23) | copy-start | bytes 196612
  116.7 10.8 %all-to-all-start.2 = ((bf16[4,128,128]{2,0,1:T(4,128)(2,1)}), bf16[4,128,128]{2,0,1:T(4,128)(2,1)S(1)}, u32[]{:S(2)}, u32[]{:S(2)}) async-start(bf16[4,128,128]{2,0,1:T(4,128)(2,1)} %copy.55), calls=%async_computation.2 | async-start | bytes 262144 | tf_op jit(solution)/shard_map/all_to_all | solution.py:41
  129.9 10.8 %all-to-all-start.3 = ((bf16[128,4,128]{2,1,0:T(4,128)(2,1)}), bf16[128,4,128]{2,1,0:T(4,128)(2,1)S(1)}, u32[]{:S(2)}, u32[]{:S(2)}) async-start(bf16[128,4,128]{2,1,0:T(4,128)(2,1)} %copy.59), calls=%async_computation.3 | async-start | bytes 262144 | tf_op jit(solution)/shard_map/all_to_all | solution.py:27
  140.7 10.8 %all-to-all-start.4 = ((bf16[128,4,128]{2,1,0:T(4,128)(2,1)}), bf16[128,4,128]{2,1,0:T(4,128)(2,1)S(1)}, u32[]{:S(2)}, u32[]{:S(2)}) async-start(bf16[128,4,128]{2,1,0:T(4,128)(2,1)} %copy.62), calls=%async_computation.4 | async-start | bytes 262144 | tf_op jit(solution)/shard_map/all_to_all | solution.py:28
  152.7 10.8 %all-to-all-start.5 = ((bf16[4,128,128]{2,0,1:T(4,128)(2,1)}), bf16[4,128,128]{2,0,1:T(4,128)(2,1)S(1)}, u32[]{:S(2)}, u32[]{:S(2)}) async-start(bf16[4,128,128]{2,0,1:T(4,128)(2,1)} %copy.66), calls=%async_computation.5 | async-start | bytes 262144 | tf_op jit(solution)/shard_map/all_to_all | solution.py:41
where the time goes:
time: 165 us
  blocking collectives  80.6 us (49%)
  waiting for transfers between devices  47.3 us (29%)
  starting transfers between devices  15.4 us (9%)
  matrix products  7.96 us (5%)
  local copies, waits for them, and re-layouts  7.48 us (5%)
  other arithmetic  5.36 us (3%)
    all_gather x1, blocking collectives, local(): lax.all_gather(right_all, 'dap', axis=1, tiled=True)  43.9 us
    all_gather x1, blocking collectives, local(): lax.all_gather(mask_all, 'dap', axis=1, tiled=True)  36.7 us
    all_to_all x2, waiting for transfers between devices, triangle(): lax.all_to_all(mixed.astype(jnp.bfloat16), 'dap', split_axis=1, concat_ax...  16.3 us
    all_to_all x2, waiting for transfers between devices, triangle(): lax.all_to_all(right_side, 'dap', split_axis=0, concat_axis=1, tiled=True)  16.2 us
    all_to_all x2, waiting for transfers between devices, triangle(): lax.all_to_all(left_side, 'dap', split_axis=0, concat_axis=1, tiled=True)  14.9 us
    all_to_all x2, starting transfers between devices, triangle(): lax.all_to_all(left_side, 'dap', split_axis=0, concat_axis=1, tiled=True)  5.15 us
    all_to_all x2, starting transfers between devices, triangle(): lax.all_to_all(mixed.astype(jnp.bfloat16), 'dap', split_axis=1, concat_ax...  5.15 us
    all_to_all x2, starting transfers between devices, triangle(): lax.all_to_all(right_side, 'dap', split_axis=0, concat_axis=1, tiled=True)  5.14 us
  transfers between devices with their start and end apart: 6, of which 6 were waited for; matrix products, arithmetic and copies ran while one was open for 1% of the time, Pallas kernels for 0%

commit v1 on v0

--- a/solution.py
+++ b/solution.py
@@ -23,10 +23,10 @@
     gating = jax.nn.sigmoid(projected_alignment[4 * width :])
     left_side = (pair_mask[None] * jax.nn.sigmoid(left_gate) * left_value).astype(jnp.bfloat16)
     right_side = (pair_mask[None] * jax.nn.sigmoid(right_gate) * right_value).astype(jnp.bfloat16)
-    left_channels, right_channels = (
-        lax.all_to_all(left_side, "dap", split_axis=0, concat_axis=1, tiled=True),
-        lax.all_to_all(right_side, "dap", split_axis=0, concat_axis=1, tiled=True),
+    both_sides = lax.all_to_all(
+        jnp.stack([left_side, right_side], axis=1), "dap", split_axis=0, concat_axis=2, tiled=True
     )
+    left_channels, right_channels = both_sides[:, 0], both_sides[:, 1]
     if outgoing:
         left_full = lax.all_gather(left_channels, "sub", axis=2, tiled=True)
         right_rows = lax.all_to_all(right_channels, "sub", split_axis=1, concat_axis=2, tiled=True)
@@ -98,10 +98,13 @@
         lax.all_gather(right_proj, "sub", axis=0, tiled=True),
         lax.all_gather(mask_bits, "sub", axis=0, tiled=True),
     )
-    right_wide, mask_wide = (
-        lax.all_gather(right_all, "dap", axis=1, tiled=True),
-        lax.all_gather(mask_all, "dap", axis=1, tiled=True),
-    )
+    packed = jnp.concatenate([right_all, mask_all], axis=1)
+    copies = jnp.broadcast_to(packed[None], (lax.axis_size("dap"),) + packed.shape)
+    arrived = lax.all_to_all(copies, "dap", split_axis=0, concat_axis=0, tiled=True)
+    arrived = jnp.transpose(arrived, (1, 0, 2))
+    right_columns = right_all.shape[1]
+    right_wide = arrived[:, :, :right_columns].reshape(arrived.shape[0], -1)
+    mask_wide = arrived[:, :, right_columns:].reshape(arrived.shape[0], -1)
     right_column_block = lax.dynamic_slice_in_dim(
         right_wide,
         sub_index * (column_halfway * outer_product_width),

time: 165 us -> 90.2 us (0.55)
  blocking collectives: 80.6 us -> 25.8 us
  waiting for transfers between devices: 47.3 us -> 31.6 us
  starting transfers between devices: 15.4 us -> 12.4 us
  local copies, waits for them, and re-layouts: 7.48 us -> 5.76 us
    all_gather x2 -> x0, blocking collectives: 80.6 us -> none  [the longest x1 43.9 us: local(): lax.all_gather(right_all, 'dap', axis=1, tiled=True)]
    all_to_all x0 -> x2, blocking collectives: none -> 25.8 us  [triangle(): lax.all_to_all(jnp.stack([left_side, right_side], axis=1), 'dap', split_a...]
    all_to_all x4 -> x1, waiting for transfers between devices: 31.1 us -> 15.3 us  [local(): lax.all_to_all(copies, 'dap', split_axis=0, concat_axis=0, tiled=True)]
    convert_element_type x4 -> x1, local copies, waits for them, and re-layouts: 3.12 us -> 0.1 us  [local(): mask_bits = mask_as_float.astype(jnp.bfloat16)]
    all_to_all x4 -> x1, starting transfers between devices: 10.3 us -> 7.29 us  [local(): lax.all_to_all(copies, 'dap', split_axis=0, concat_axis=0, tiled=True)]
  transfers between devices with their start and end apart: 6 -> 3, of which waited for: 6 -> 3; matrix products, arithmetic and copies ran while one was open for 1% -> 0% of each run, Pallas kernels for 0% -> 0%
where the time goes in v1:
time: 90.2 us; the launch traced here: 89.5 us
  waiting for transfers between devices  31.6 us (35%)
  blocking collectives  25.8 us (29%)
  starting transfers between devices  12.4 us (14%)
  matrix products  7.99 us (9%)
  local copies, waits for them, and re-layouts  5.76 us (6%)
  other arithmetic  5.45 us (6%)
    all_to_all x2, blocking collectives, triangle(): lax.all_to_all(jnp.stack([left_side, right_side], axis=1), 'dap', split_a...  25.8 us
    all_to_all x2, waiting for transfers between devices, triangle(): lax.all_to_all(mixed.astype(jnp.bfloat16), 'dap', split_axis=1, concat_ax...  16.3 us
    all_to_all x1, waiting for transfers between devices, local(): lax.all_to_all(copies, 'dap', split_axis=0, concat_axis=0, tiled=True)  15.3 us
    all_to_all x1, starting transfers between devices, local(): lax.all_to_all(copies, 'dap', split_axis=0, concat_axis=0, tiled=True)  7.29 us
    all_to_all x2, starting transfers between devices, triangle(): lax.all_to_all(mixed.astype(jnp.bfloat16), 'dap', split_axis=1, concat_ax...  5.15 us
    dot_general x4, matrix products, opm_row(): jnp.dot(outer_prod, outer_output_weight, preferred_element_type=jnp.float32)  4.21 us
  transfers between devices with their start and end apart: 3, of which 3 were waited for; matrix products, arithmetic and copies ran while one was open for 0% of the time, Pallas kernels for 0%

profile of v1, /device:TPU:0, one launch (start us, length us, event | category | flops | bytes accessed | tf_op | source)
XLA Modules:
  0.0 89.5 jit_solution(16058506339619712919)
XLA Ops:
  0.0 1.0 %convert_reduce_fusion.1 = f32[32,4]{1,0:T(8,128)S(1)} fusion(bf16[32,4,256]{2,1,0:T(4,128)(2,1)} %param.13), kind=kLoop, calls=%fused_computation.92 | loop fusion | flops 65408 | bytes 66048 | tf_op jit(solution)/shard_map/reduce_sum | solution.py:8
  1.0 1.0 %fusion.65 = f32[32,4]{1,0:T(8,128)S(1)} fusion(bf16[32,4,256]{2,1,0:T(4,128)(2,1)} %param.13, f32[32,4]{1,0:T(8,128)S(1)} %broadcast_multiply_fusion), kind=kLoop, calls=%fused_computation.99 | loop fusion | flops 130944 | bytes 66560 | tf_op jit(solution)/shard_map/reduce_sum | solution.py:9
  2.1 0.7 convert_convert_fusion
  2.7 1.0 %fusion.67 = bf16[32,4,256]{2,1,0:T(4,128)(2,1)S(1)} fusion(bf16[32,4,256]{2,1,0:T(4,128)(2,1)} %param.13, f32[256]{0:T(256)} %param.17, f32[32,4]{1,0:T(8,128)S(1)} %add_rsqrt_fusion, f32[32,4]{1,0:T(8,128)S(1)} %broadcast_multiply_fusion), kind=kLoop, calls=%fused_computation.101 | loop fusion | flops 163840 | bytes 133120 | tf_op jit(solution)/shard_map/convert_element_type | solution.py:74
  4.2 0.9 broadcast_in_dim.8
  5.1 7.3 %all-to-all-start = ((bf16[32,32,132]{2,1,0:T(8,128)(2,1)}), bf16[32,32,132]{2,1,0:T(8,128)(2,1)S(1)}, u32[]{:S(2)}, u32[]{:S(2)}) async-start(bf16[32,32,132]{2,1,0:T(8,128)(2,1)} %broadcast_in_dim.8), calls=%async_computation | async-start | bytes 1048576 | tf_op jit(solution)/shard_map/all_to_all | solution.py:103
  12.6 15.3 %all-to-all-done = bf16[32,32,132]{2,1,0:T(8,128)(2,1)S(1)} async-done(((bf16[32,32,132]{2,1,0:T(8,128)(2,1)}), bf16[32,32,132]{2,1,0:T(8,128)(2,1)S(1)}, u32[]{:S(2)}, u32[]{:S(2)}) %all-to-all-start) | async-done | bytes 270368 | tf_op jit(solution)/shard_map/all_to_all | solution.py:103
  28.6 0.4 reshape.132
  29.0 0.5 copy.74
  29.6 5.8 %while.10 = (s32[]{:T(128)}, bf16[4,128,128]{2,1,0:T(8,128)(2,1)S(1)}, bf16[4,128,128]{2,1,0:T(8,128)(2,1)}, bf16[4,32,32]{2,1,0:T(8,128)(2,1)S(1)}, bf16[32,128...) while((s32[]{:T(128)}, ...), condition=%wide.region_3.4_spmd, body=%wide.region_2.3_spmd.sunk | while | flops 42156160 | bytes 1648745 | solution.py:141
  30.0 1.1 %fusion.107 = bf16[4,128,128]{2,1,0:T(8,128)(2,1)S(1)} fusion(bf16[4,128,128]{2,1,0:T(8,128)(2,1)S(1)} %get-tuple-element.171, s32[]{:T(128)} %get-tuple-element.170, bf16[128,1024]{0,1:T(8,128)(2,1)S(1)} %bitcast.174, bf16[1024,128]{1,0:T(8,128)(2,1)S(1)} %get-tuple-element.184, f32[128]{0:T(128)S(1)} %fusion.106, f32[128]{0:T(128)S(1)} %get-tuple-element.185, ...), kind=kOutput, calls=%fused_computation.7.clone.1 | convolution fusion | flops 33636352 | bytes 590852 | tf_op jit(solution)/shard_map/while/body/eval_jaxpr/dot_general | solution.py:134
  31.4 1.1 %fusion.107 = bf16[4,128,128]{2,1,0:T(8,128)(2,1)S(1)} fusion(bf16[4,128,128]{2,1,0:T(8,128)(2,1)S(1)} %get-tuple-element.171, s32[]{:T(128)} %get-tuple-element.170, bf16[128,1024]{0,1:T(8,128)(2,1)S(1)} %bitcast.174, bf16[1024,128]{1,0:T(8,128)(2,1)S(1)} %get-tuple-element.184, f32[128]{0:T(128)S(1)} %fusion.106, f32[128]{0:T(128)S(1)} %get-tuple-element.185, ...), kind=kOutput, calls=%fused_computation.7.clone.1 | convolution fusion | flops 33636352 | bytes 590852 | tf_op jit(solution)/shard_map/while/body/eval_jaxpr/dot_general | solution.py:134
  32.9 1.1 %fusion.107 = bf16[4,128,128]{2,1,0:T(8,128)(2,1)S(1)} fusion(bf16[4,128,128]{2,1,0:T(8,128)(2,1)S(1)} %get-tuple-element.171, s32[]{:T(128)} %get-tuple-element.170, bf16[128,1024]{0,1:T(8,128)(2,1)S(1)} %bitcast.174, bf16[1024,128]{1,0:T(8,128)(2,1)S(1)} %get-tuple-element.184, f32[128]{0:T(128)S(1)} %fusion.106, f32[128]{0:T(128)S(1)} %get-tuple-element.185, ...), kind=kOutput, calls=%fused_computation.7.clone.1 | convolution fusion | flops 33636352 | bytes 590852 | tf_op jit(solution)/shard_map/while/body/eval_jaxpr/dot_general | solution.py:134
  34.3 1.1 %fusion.107 = bf16[4,128,128]{2,1,0:T(8,128)(2,1)S(1)} fusion(bf16[4,128,128]{2,1,0:T(8,128)(2,1)S(1)} %get-tuple-element.171, s32[]{:T(128)} %get-tuple-element.170, bf16[128,1024]{0,1:T(8,128)(2,1)S(1)} %bitcast.174, bf16[1024,128]{1,0:T(8,128)(2,1)S(1)} %get-tuple-element.184, f32[128]{0:T(128)S(1)} %fusion.106, f32[128]{0:T(128)S(1)} %get-tuple-element.185, ...), kind=kOutput, calls=%fused_computation.7.clone.1 | convolution fusion | flops 33636352 | bytes 590852 | tf_op jit(solution)/shard_map/while/body/eval_jaxpr/dot_general | solution.py:134
  36.6 13.5 %all_to_all.59 = bf16[128,2,4,128]{3,2,1,0:T(4,128)(2,1)S(1)} all-to-all(bf16[128,2,4,128]{3,2,1,0:T(4,128)(2,1)S(1)} %copy.75), channel_id=1, replica_groups=mesh['grp'=1,'dap'=32,'sub'=1] {'dap'}, dimensions={0} | all-to-all | bytes 524288 | tf_op jit(solution)/shard_map/all_to_all | solution.py:26
  50.6 0.8 copy.78
  51.3 2.6 %all-to-all-start.2 = ((bf16[4,128,128]{2,0,1:T(4,128)(2,1)}), bf16[4,128,128]{2,0,1:T(4,128)(2,1)S(1)}, u32[]{:S(2)}, u32[]{:S(2)}) async-start(bf16[4,128,128]{2,0,1:T(4,128)(2,1)} %copy.78), calls=%async_computation.2 | async-start | bytes 262144 | tf_op jit(solution)/shard_map/all_to_all | solution.py:41
  54.0 8.1 %all-to-all-done.2 = bf16[4,128,128]{2,0,1:T(4,128)(2,1)S(1)} async-done(((bf16[4,128,128]{2,0,1:T(4,128)(2,1)}), bf16[4,128,128]{2,0,1:T(4,128)(2,1)S(1)}, u32[]{:S(2)}, u32[]{:S(2)}) %all-to-all-start.2) | async-done | bytes 131104 | tf_op jit(solution)/shard_map/all_to_all | solution.py:41
  63.1 0.4 convolution_bitcast_fusion
  64.0 12.3 %all_to_all.60 = bf16[128,2,4,128]{3,2,1,0:T(4,128)(2,1)S(1)} all-to-all(bf16[128,2,4,128]{3,2,1,0:T(4,128)(2,1)S(1)} %copy.82), channel_id=1, replica_groups=mesh['grp'=1,'dap'=32,'sub'=1] {'dap'}, dimensions={0} | all-to-all | bytes 524288 | tf_op jit(solution)/shard_map/all_to_all | solution.py:26
  76.8 0.8 copy.86
  77.5 2.6 %all-to-all-start.4 = ((bf16[4,128,128]{2,0,1:T(4,128)(2,1)}), bf16[4,128,128]{2,0,1:T(4,128)(2,1)S(1)}, u32[]{:S(2)}, u32[]{:S(2)}) async-start(bf16[4,128,128]{2,0,1:T(4,128)(2,1)} %copy.86), calls=%async_computation.4 | async-start | bytes 262144 | tf_op jit(solution)/shard_map/all_to_all | solution.py:41
  80.2 8.1 %all-to-all-done.4 = bf16[4,128,128]{2,0,1:T(4,128)(2,1)S(1)} async-done(((bf16[4,128,128]{2,0,1:T(4,128)(2,1)}), bf16[4,128,128]{2,0,1:T(4,128)(2,1)S(1)}, u32[]{:S(2)}, u32[]{:S(2)}) %all-to-all-start.4) | async-done | bytes 131104 | tf_op jit(solution)/shard_map/all_to_all | solution.py:41
  88.7 0.9 fusion.19
  (79 shorter events, 6.7 us)
Async XLA Ops:
  0.0 3.7 %copy-start = (bf16[256,64]{0,1:T(8,128)(2,1)S(1)}, bf16[256,64]{0,1:T(8,128)(2,1)}, u32[]{:S(2)}) copy-start(bf16[256,64]{0,1:T(8,128)(2,1)} %param.18) | copy-start | bytes 98308
  0.0 12.4 %copy-start.5 = (s32[128]{0:T(128)S(1)}, s32[128]{0:T(128)}, u32[]{:S(2)}) copy-start(s32[128]{0:T(128)} %param.16) | copy-start | bytes 1540
  0.0 12.5 %copy-start.2 = (f32[4,128]{1,0:T(4,128)S(1)}, f32[4,128]{1,0:T(4,128)}, u32[]{:S(2)}) copy-start(f32[4,128]{1,0:T(4,128)} %param.21) | copy-start | bytes 6148
  5.1 22.8 %all-to-all-start = ((bf16[32,32,132]{2,1,0:T(8,128)(2,1)}), bf16[32,32,132]{2,1,0:T(8,128)(2,1)S(1)}, u32[]{:S(2)}, u32[]{:S(2)}) async-start(bf16[32,32,132]{2,1,0:T(8,128)(2,1)} %broadcast_in_dim.8), calls=%async_computation | async-start | bytes 1048576 | tf_op jit(solution)/shard_map/all_to_all | solution.py:103
  28.5 1.0 %copy-start.3 = (bf16[1024,128]{1,0:T(8,128)(2,1)S(1)}, bf16[1024,128]{1,0:T(8,128)(2,1)}, u32[]{:S(2)}) copy-start(bf16[1024,128]{1,0:T(8,128)(2,1)} %param.19) | copy-start | bytes 786436
  28.6 1.0 %copy-start.6 = (f32[128]{0:T(128)S(1)}, f32[128]{0:T(128)}, u32[]{:S(2)}) copy-start(f32[128]{0:T(128)} %param.20) | copy-start | bytes 1540
  29.6 6.2 %copy-start.1 = (bf16[2,128,640]{2,1,0:T(8,128)(2,1)S(1)}, bf16[2,128,640]{2,1,0:T(8,128)(2,1)}, u32[]{:S(2)}) copy-start(bf16[2,128,640]{2,1,0:T(8,128)(2,1)} %param.22) | copy-start | bytes 983044
  50.1 12.4 %copy-start.4 = (bf16[2,128,128]{2,1,0:T(8,128)(2,1)S(1)}, bf16[2,128,128]{2,1,0:T(8,128)(2,1)}, u32[]{:S(2)}) copy-start(bf16[2,128,128]{2,1,0:T(8,128)(2,1)} %param.23) | copy-start | bytes 196612
  51.3 10.8 %all-to-all-start.2 = ((bf16[4,128,128]{2,0,1:T(4,128)(2,1)}), bf16[4,128,128]{2,0,1:T(4,128)(2,1)S(1)}, u32[]{:S(2)}, u32[]{:S(2)}) async-start(bf16[4,128,128]{2,0,1:T(4,128)(2,1)} %copy.78), calls=%async_computation.2 | async-start | bytes 262144 | tf_op jit(solution)/shard_map/all_to_all | solution.py:41
  77.5 10.8 %all-to-all-start.4 = ((bf16[4,128,128]{2,0,1:T(4,128)(2,1)}), bf16[4,128,128]{2,0,1:T(4,128)(2,1)S(1)}, u32[]{:S(2)}, u32[]{:S(2)}) async-start(bf16[4,128,128]{2,0,1:T(4,128)(2,1)} %copy.86), calls=%async_computation.4 | async-start | bytes 262144 | tf_op jit(solution)/shard_map/all_to_all | solution.py:41

commit v2 on v1

--- a/solution.py
+++ b/solution.py
@@ -1,6 +1,10 @@
+import functools
+
 import jax
 import jax.numpy as jnp
 from jax import lax
+from jax.experimental import pallas as pl
+from jax.experimental.pallas import tpu as pltpu
 from jax.sharding import PartitionSpec as P
 
 
@@ -158,9 +162,275 @@
     return current
 
 
+F32, BF16 = jnp.float32, jnp.bfloat16
+MESH = pl.DeviceIdType.MESH
+LANES = 128
+
+
+def dot(a, b, da, db):
+    return lax.dot_general(a, b, (((da,), (db,)), ((), ())), preferred_element_type=F32)
+
+
+def exchange(n, me, source, arrived, send_sem, recv_sem):
+    def start(offset, carry):
+        peer = lax.rem(me + offset, n)
+        pltpu.make_async_remote_copy(
+            src_ref=source(peer),
+            dst_ref=arrived.at[me],
+            send_sem=send_sem,
+            recv_sem=recv_sem,
+            device_id={"dap": peer},
+            device_id_type=MESH,
+        ).start()
+        return carry
+
+    lax.fori_loop(1, n, start, 0)
+
+
+def await_bytes(n, arrived, sem):
+    others = arrived.at[pl.ds(0, n - 1)]
+    pltpu.make_async_copy(others, others, sem).wait()
+
+
+def fused_kernel(
+    n,
+    rows,
+    depth,
+    x_ref,
+    mask_ref,
+    pair_ref,
+    seq_ref,
+    scale_ref,
+    map_ref,
+    outer_ref,
+    bias_ref,
+    gains_ref,
+    w_in_ref,
+    w_out_ref,
+    out_ref,
+    send_a,
+    recv_a,
+    send_b,
+    recv_b,
+    send_c,
+    recv_c,
+    wide,
+    first,
+    second,
+    mixed_rows,
+    factors,
+    w_turned,
+    sems,
+):
+    me = lax.axis_index("dap")
+    barrier = pltpu.get_barrier_semaphore()
+
+    def greet(offset, carry):
+        pl.semaphore_signal(
+            barrier, inc=1, device_id={"dap": lax.rem(me + offset, n)}, device_id_type=MESH
+        )
+        return carry
+
+    lax.fori_loop(1, n, greet, 0)
+
+    width = pair_ref.shape[2]
+    tensor = map_ref.shape[1] // 2
+    per = width // n
+    strip = rows * per
+    blocks = tensor * depth // LANES
+    high = tensor // blocks
+
+    normed = apply_layer_norm(x_ref[...].astype(F32), scale_ref[...], 1).astype(BF16)
+    mask_col = mask_ref[...].astype(F32)
+    proj = dot(normed, map_ref[...], 1, 0) * mask_col
+    left = proj[:, :tensor].astype(BF16)
+    turned = jnp.concatenate(
+        [proj, jnp.broadcast_to(mask_col, (rows * depth, LANES - 2 * tensor))], axis=1
+    ).T
+    pieces = []
+    for j in range(rows):
+        lanes = slice(j * depth, (j + 1) * depth)
+        pieces.append(
+            jnp.concatenate(
+                [
+                    turned[tensor + h * blocks : tensor + (h + 1) * blocks, lanes]
+                    for h in range(high)
+                ],
+                axis=1,
+            )
+        )
+    row_of = lax.broadcasted_iota(jnp.int32, (4 * rows, depth), 0) // 4
+    mask_rows = jnp.zeros((4 * rows, depth), F32)
+    for j in range(rows):
+        spread = turned[2 * tensor : 2 * tensor + 4 * rows, j * depth : (j + 1) * depth]
+        mask_rows = jnp.where(row_of == j, spread, mask_rows)
+    mask_rows = jnp.concatenate([mask_rows, jnp.zeros((4 * rows, LANES - depth), F32)], axis=1)
+    packed = jnp.concatenate(pieces + [mask_rows], axis=0).astype(BF16)
+    send_a[...] = packed
+    recv_a[me] = packed
+    pl.semaphore_wait(barrier, n - 1)
+    exchange(n, me, lambda peer: send_a, recv_a, sems.at[0], sems.at[1])
+
+    wide[...] = outer_ref[...].astype(F32)
+    for q in range(tensor):
+        weight = wide[pl.ds(q, tensor, stride=tensor), :].astype(BF16)
+        factor = dot(left, weight, 1, 0).astype(BF16)
+        place = (q % blocks) * LANES + (q // blocks) * depth
+        for i in range(rows):
+            factors[place : place + depth, i * width : (i + 1) * width] = factor[
+                i * depth : (i + 1) * depth
+            ]
+    for t in range(2):
+        w_turned[t] = w_in_ref[t, :, : 4 * width].astype(F32).T.astype(BF16)
+    seq = seq_ref[...].astype(F32)
+    lane = lax.broadcasted_iota(jnp.int32, seq.shape, 1)
+    pair_mask = jnp.concatenate(
+        [
+            seq * jnp.sum(jnp.where(lane == me * rows + r, seq, 0.0), 1, keepdims=True)
+            for r in range(rows)
+        ],
+        axis=1,
+    )
+
+    await_bytes(n, recv_a, sems.at[1])
+    total = n * rows
+    kept = rows * blocks
+    wide[...] = recv_a[:, :kept, :].astype(F32).reshape(n * kept, LANES)
+    first[...] = recv_a[:, kept:, :].astype(F32).reshape(4 * total, LANES)
+    right = jnp.concatenate(
+        [wide[pl.ds(b, total, stride=blocks), :].astype(BF16) for b in range(blocks)], axis=1
+    )
+    mask_all = first[pl.ds(0, total, stride=4), :][:, :depth].astype(BF16)
+    values = dot(right, factors[...], 1, 0)
+    current = []
+    for i in range(rows):
+        own = jnp.broadcast_to(mask_col[i * depth : (i + 1) * depth], (depth, width)).astype(BF16)
+        counts = dot(mask_all, own, 1, 0)
+        update = (values[:, i * width : (i + 1) * width] + bias_ref[...]) / jnp.maximum(counts, 1.0)
+        current.append((pair_ref[i].astype(F32) + update).astype(BF16))
+
+    for t in range(2):
+        z = jnp.concatenate([row.astype(F32) for row in current], axis=0)
+        normed = apply_layer_norm(z, gains_ref[2 * t : 2 * t + 1, :], 1).astype(BF16)
+        turned = dot(w_turned[t], normed, 1, 1)
+        for side, scratch in ((0, first), (1, second)):
+            value = turned[side * width : (side + 1) * width]
+            gate = turned[(2 + side) * width : (3 + side) * width]
+            gated = pair_mask * jax.nn.sigmoid(gate) * value
+            for r in range(rows):
+                scratch[r * width : (r + 1) * width, :] = gated[:, r * total : (r + 1) * total]
+        for d in range(n):
+            send_b[t, d, :strip, :] = first[pl.ds(d, strip, stride=n), :].astype(BF16)
+            send_b[t, d, strip:, :] = second[pl.ds(d, strip, stride=n), :].astype(BF16)
+        s = 2 + 4 * t
+        exchange(n, me, lambda peer: send_b.at[t, peer], recv_b.at[t], sems.at[s], sems.at[s + 1])
+        recv_b[t, me] = send_b[t, me]
+        gating = jax.nn.sigmoid(dot(normed, w_in_ref[t, :, 4 * width :], 1, 0))
+        gain = jnp.broadcast_to(gains_ref[2 * t + 1 : 2 * t + 2, :], (total, width)).T
+        await_bytes(n, recv_b.at[t], sems.at[s + 1])
+        first[...] = recv_b[t, :, :strip, :].astype(F32).reshape(n * strip, LANES)
+        second[...] = recv_b[t, :, strip:, :].astype(F32).reshape(n * strip, LANES)
+        for c in range(per):
+            one = first[pl.ds(c, total, stride=per), :].astype(BF16)
+            two = second[pl.ds(c, total, stride=per), :].astype(BF16)
+            over = 1 - t
+            mixed_rows[pl.ds(c, total, stride=per), :] = dot(one, two, over, over)
+        send_c[t] = mixed_rows[...].astype(BF16).reshape(n, strip, LANES)
+        exchange(n, me, lambda peer: send_c.at[t, peer], recv_c.at[t], sems.at[s + 2], sems.at[s + 3])
+        recv_c[t, me] = send_c[t, me]
+        await_bytes(n, recv_c.at[t], sems.at[s + 3])
+        first[...] = recv_c[t].astype(F32).reshape(n * strip, LANES)
+        following = []
+        for r in range(rows):
+            mixed = jnp.concatenate(
+                [first[pl.ds(r * per + c, n, stride=strip), :] for c in range(per)], axis=0
+            )
+            mixed_norm = apply_layer_norm(mixed, gain, 0).astype(BF16)
+            update = dot(mixed_norm, w_out_ref[t], 0, 0)
+            block = slice(r * total, (r + 1) * total)
+            following.append((z[block] + gating[block] * update).astype(BF16))
+        current = following
+    for r in range(rows):
+        out_ref[r] = current[r]
+    await_bytes(n, recv_a, sems.at[0])
+    for t in range(2):
+        await_bytes(n, recv_b.at[t], sems.at[2 + 4 * t])
+        await_bytes(n, recv_c.at[t], sems.at[4 + 4 * t])
+
+
+def fused(
+    n,
+    homolog_embedding,
+    alignment_mask,
+    pair_activation,
+    sequence_mask,
+    homolog_scaling_factor,
+    homolog_mapping_matrix,
+    outer_output_weight,
+    outer_output_bias,
+    pair_norm_gains,
+    triangle_input_weights,
+    triangle_output_weights,
+):
+    depth, rows, channels = homolog_embedding.shape
+    total, width = pair_activation.shape[1:]
+    strip = rows * (width // n)
+    outer = outer_output_weight.shape[0]
+    kept = rows * (homolog_mapping_matrix.shape[1] // 2) * depth // LANES
+    vmem = pl.BlockSpec(memory_space=pltpu.VMEM)
+    return pl.pallas_call(
+        functools.partial(fused_kernel, n, rows, depth),
+        out_shape=jax.ShapeDtypeStruct(pair_activation.shape, BF16),
+        in_specs=[vmem] * 11,
+        out_specs=vmem,
+        scratch_shapes=[
+            pltpu.VMEM((kept + 4 * rows, LANES), BF16),
+            pltpu.VMEM((n, kept + 4 * rows, LANES), BF16),
+            pltpu.VMEM((2, n, 2 * strip, total), BF16),
+            pltpu.VMEM((2, n, 2 * strip, total), BF16),
+            pltpu.VMEM((2, n, strip, total), BF16),
+            pltpu.VMEM((2, n, strip, total), BF16),
+            pltpu.VMEM((outer, width), F32),
+            pltpu.VMEM((rows * width, LANES), F32),
+            pltpu.VMEM((rows * width, LANES), F32),
+            pltpu.VMEM((rows * width, LANES), F32),
+            pltpu.VMEM((outer, rows * width), BF16),
+            pltpu.VMEM((2, 4 * width, width), BF16),
+            pltpu.SemaphoreType.DMA((10,)),
+        ],
+        compiler_params=pltpu.CompilerParams(
+            collective_id=0, has_side_effects=True, vmem_limit_bytes=40 * 1024 * 1024
+        ),
+    )(
+        jnp.transpose(homolog_embedding, (1, 0, 2)).reshape(rows * depth, channels),
+        jnp.transpose(alignment_mask).reshape(rows * depth, 1),
+        pair_activation,
+        sequence_mask.reshape(1, total),
+        homolog_scaling_factor.reshape(1, channels),
+        homolog_mapping_matrix,
+        outer_output_weight,
+        outer_output_bias.reshape(1, width),
+        pair_norm_gains,
+        triangle_input_weights,
+        triangle_output_weights,
+    )
+
+
 def solution(mesh):
+    n, sub = mesh.shape["dap"], mesh.shape["sub"]
+
+    def chosen(*arrays):
+        depth, rows, _ = arrays[0].shape
+        total, width = arrays[2].shape[1:]
+        tensor = arrays[5].shape[1] // 2
+        fits = (
+            sub == 1
+            and (depth, rows, total, width, tensor) == (32, 4, LANES, LANES, 32)
+            and n * rows == total
+        )
+        return fused(n, *arrays) if fits else local(*arrays)
     return jax.shard_map(
-        local,
+        chosen,
         mesh=mesh,
         in_specs=(
             P(("grp", "sub"), "dap", None),

time: 90.2 us -> 52.9 us (0.59)
  Pallas kernels: 0 us -> 46.5 us
  waiting for transfers between devices: 31.6 us -> 0 us
  blocking collectives: 25.8 us -> 0 us
  starting transfers between devices: 12.4 us -> 0 us
  matrix products: 7.99 us -> 0 us
  other arithmetic: 5.45 us -> 0 us
    pallas_call x0 -> x1, Pallas kernels: none -> 46.5 us  [fused(): pl.pallas_call(functools.partial(fused_kernel, n, rows, depth), out_shape...]
    all_to_all x3 -> x0, waiting for transfers between devices: 31.6 us -> none  [the longest x2 16.3 us: triangle(): lax.all_to_all(mixed.astype(jnp.bfloat16), 'dap', split_axis=1, concat_ax...]
    all_to_all x2 -> x0, blocking collectives: 25.8 us -> none  [triangle(): lax.all_to_all(jnp.stack([left_side, right_side], axis=1), 'dap', split_a...]
    all_to_all x3 -> x0, starting transfers between devices: 12.4 us -> none  [the longest x1 7.29 us: local(): lax.all_to_all(copies, 'dap', split_axis=0, concat_axis=0, tiled=True)]
    dot_general x16 -> x0, matrix products: 7.99 us -> none  [the longest x4 4.21 us: opm_row(): jnp.dot(outer_prod, outer_output_weight, preferred_element_type=jnp.float32)]
    unnamed x14 -> x18, local copies, waits for them, and re-layouts: 0.03 us -> 4.28 us
    reduce_sum x9 -> x0, other arithmetic: 2.94 us -> none  [the longest x5 1.71 us: apply_layer_norm(): spread = jnp.mean(center * center, dimension, keepdims=True)]
    convert_element_type x8 -> x0, local copies, waits for them, and re-layouts: 2.09 us -> none  [the longest x2 1.52 us: triangle(): mixed.astype(jnp.bfloat16)]
  transfers between devices with their start and end apart: 3 -> 0, of which waited for: 3 -> 0; matrix products, arithmetic and copies ran while one was open for 0% -> 0% of each run, Pallas kernels for 0% -> 0%
where the time goes in v2:
time: 52.9 us; the launch traced here: 52.6 us
  Pallas kernels  46.5 us (88%)
  local copies, waits for them, and re-layouts  5.96 us (11%)
    pallas_call x1, Pallas kernels, fused(): pl.pallas_call(functools.partial(fused_kernel, n, rows, depth), out_shape...  46.5 us
    unnamed x18, local copies, waits for them, and re-layouts  4.28 us

profile of v2, /device:TPU:0, one launch (start us, length us, event | category | flops | bytes accessed | tf_op | source)
XLA Modules:
  0.0 52.6 jit_solution(13883580232904628172)
XLA Ops:
  0.0 0.0 copy-start.1
  0.0 0.9 %copy.12 = bf16[4,32,256]{2,1,0:T(8,128)(2,1)S(1)} copy(bf16[4,32,256]{2,0,1:T(4,128)(2,1)} %bitcast.10) | data formatting | bytes 131072 | tf_op jit(solution)/shard_map/transpose | solution.py:405
  0.9 0.8 %reshape.20.mask_ref = s32[128,1]{1,0:T(8,128)S(1)} reshape(s32[4,32]{1,0:T(4,128)} %bitcast.11) | data formatting | bytes 1024 | tf_op jit(solution)/shard_map/reshape | solution.py:406
  1.7 0.0 copy-start.4
  1.7 0.0 copy-start.5
  1.7 0.0 copy-start.6
  1.7 0.0 copy-start.7
  1.7 0.9 %copy.14.map_ref = bf16[256,64]{1,0:T(8,128)(2,1)S(1)} copy(bf16[256,64]{0,1:T(8,128)(2,1)} %param.16) | data formatting | bytes 65536 | tf_op args[5]
  2.6 0.0 copy-done.1
  2.6 0.0 copy-done.4
  2.6 0.0 copy-done.5
  2.7 0.0 copy-done.6
  2.7 0.0 copy-done.7
  2.7 0.0 copy-start
  2.7 1.0 %copy-done = bf16[2,128,640]{2,1,0:T(8,128)(2,1)S(1)} copy-done((bf16[2,128,640]{2,1,0:T(8,128)(2,1)S(1)}, bf16[2,128,640]{2,1,0:T(8,128)(2,1)}, u32[]{:S(2)}) %copy-start) | copy-done | bytes 327704
  3.7 0.0 copy-start.2
  3.7 0.9 %copy-done.2 = bf16[4,128,128]{2,1,0:T(8,128)(2,1)S(1)} copy-done((bf16[4,128,128]{2,1,0:T(8,128)(2,1)S(1)}, bf16[4,128,128]{2,1,0:T(8,128)(2,1)}, u32[]{:S(2)}) %copy-start.2) | copy-done | bytes 131096
  4.6 0.0 copy-start.3
  4.6 0.8 %copy-done.3 = bf16[2,128,128]{2,1,0:T(8,128)(2,1)S(1)} copy-done((bf16[2,128,128]{2,1,0:T(8,128)(2,1)S(1)}, bf16[2,128,128]{2,1,0:T(8,128)(2,1)}, u32[]{:S(2)}) %copy-start.3) | copy-done | bytes 65560
  5.4 46.5 %shard_map.109 = bf16[4,128,128]{2,1,0:T(8,128)(2,1)S(1)} custom-call(bf16[128,256]{1,0:T(8,128)(2,1)S(1)} %bitcast.6, s32[128,1]{1,0:T(8,128)S(1)} %reshape.20.mask_ref, bf16[4,128,128]{2,1,0:T(8,128)(2,1)S(1)} %copy-done.2, s32[1,128]{1,0:T(1,128)S(1)} %bitcast.8, f32[1,256]{1,0:T(1,128)S(1)} %bitcast.7, bf16[256,64]{1,0:T(8,128)(2,1)S(1)} %copy.14.map_ref, ...), custom_call_target="tpu_custom_call" | custom-call | tf_op jit(solution)/shard_map/pallas_call | solution.py:381
  51.9 0.7 %copy.16 = bf16[4,128,128]{2,1,0:T(8,128)(2,1)} copy(bf16[4,128,128]{2,1,0:T(8,128)(2,1)S(1)} %shard_map.109) | data formatting | bytes 262144
Async XLA Ops:
  0.0 2.6 %copy-start.1 = (bf16[1024,128]{1,0:T(8,128)(2,1)S(1)}, bf16[1024,128]{1,0:T(8,128)(2,1)}, u32[]{:S(2)}) copy-start(bf16[1024,128]{1,0:T(8,128)(2,1)} %outer_ref.1) | copy-start | bytes 786436
  1.7 1.0 %copy-start.4 = (f32[4,128]{1,0:T(4,128)S(1)}, f32[4,128]{1,0:T(4,128)}, u32[]{:S(2)}) copy-start(f32[4,128]{1,0:T(4,128)} %gains_ref.1) | copy-start | bytes 6148
  1.7 0.9 %copy-start.5 = (f32[256]{0:T(256)S(1)}, f32[256]{0:T(256)}, u32[]{:S(2)}) copy-start(f32[256]{0:T(256)} %param.15) | copy-start | bytes 3076
  1.7 0.9 %copy-start.6 = (s32[128]{0:T(128)S(1)}, s32[128]{0:T(128)}, u32[]{:S(2)}) copy-start(s32[128]{0:T(128)} %param.14) | copy-start | bytes 1540
  1.7 0.9 %copy-start.7 = (f32[128]{0:T(128)S(1)}, f32[128]{0:T(128)}, u32[]{:S(2)}) copy-start(f32[128]{0:T(128)} %param.18) | copy-start | bytes 1540
  2.7 1.0 %copy-start = (bf16[2,128,640]{2,1,0:T(8,128)(2,1)S(1)}, bf16[2,128,640]{2,1,0:T(8,128)(2,1)}, u32[]{:S(2)}) copy-start(bf16[2,128,640]{2,1,0:T(8,128)(2,1)} %w_in_ref.1) | copy-start | bytes 983044
  3.7 0.9 %copy-start.2 = (bf16[4,128,128]{2,1,0:T(8,128)(2,1)S(1)}, bf16[4,128,128]{2,1,0:T(8,128)(2,1)}, u32[]{:S(2)}) copy-start(bf16[4,128,128]{2,1,0:T(8,128)(2,1)} %pair_ref.1) | copy-start | bytes 393220
  4.6 0.8 %copy-start.3 = (bf16[2,128,128]{2,1,0:T(8,128)(2,1)S(1)}, bf16[2,128,128]{2,1,0:T(8,128)(2,1)}, u32[]{:S(2)}) copy-start(bf16[2,128,128]{2,1,0:T(8,128)(2,1)} %w_out_ref.1) | copy-start | bytes 196612

commit v3 on v2

--- a/solution.py
+++ b/solution.py
@@ -208,7 +208,6 @@
     w_in_ref,
     w_out_ref,
     out_ref,
-    send_a,
     recv_a,
     send_b,
     recv_b,
@@ -221,28 +220,52 @@
     factors,
     w_turned,
     sems,
+    gather_sems,
 ):
     me = lax.axis_index("dap")
     barrier = pltpu.get_barrier_semaphore()
 
-    def greet(offset, carry):
-        pl.semaphore_signal(
-            barrier, inc=1, device_id={"dap": lax.rem(me + offset, n)}, device_id_type=MESH
-        )
-        return carry
-
-    lax.fori_loop(1, n, greet, 0)
+    far, chip, core = me // 8, lax.rem(me // 2, 4), lax.rem(me, 2)
+    far_peers = [lax.rem(me + 8 * p, n) for p in range(1, 4)]
+    chip_peers = [far * 8 + lax.rem(chip + p, 4) * 2 + core for p in range(1, 4)]
+    core_peers = [me + 1 - 2 * core]
+    stages = (
+        (far_peers, core * 16 + chip * 4 + far, 1),
+        (chip_peers, core * 16 + chip * 4, 4),
+        (core_peers, core * 16, 16),
+    )
+    for peer in far_peers + chip_peers + core_peers:
+        pl.semaphore_signal(barrier, inc=1, device_id={"dap": peer}, device_id_type=MESH)
+
+    def forward(stage):
+        peers, slot, count = stages[stage]
+        held = recv_a.at[pl.ds(slot, count)]
+        for peer in peers:
+            pltpu.make_async_remote_copy(
+                src_ref=held,
+                dst_ref=held,
+                send_sem=gather_sems.at[0, stage],
+                recv_sem=gather_sems.at[1, stage],
+                device_id={"dap": peer},
+                device_id_type=MESH,
+            ).start()
+
+    def gathered(stage, way):
+        blocks_moved = recv_a.at[pl.ds(0, len(stages[stage][0]) * stages[stage][2])]
+        pltpu.make_async_copy(blocks_moved, blocks_moved, gather_sems.at[way, stage]).wait()
 
     width = pair_ref.shape[2]
-    tensor = map_ref.shape[1] // 2
+    tensor = map_ref.shape[0] // 2
     per = width // n
     strip = rows * per
     blocks = tensor * depth // LANES
     high = tensor // blocks
 
     normed = apply_layer_norm(x_ref[...].astype(F32), scale_ref[...], 1).astype(BF16)
-    mask_col = mask_ref[...].astype(F32)
-    proj = dot(normed, map_ref[...], 1, 0) * mask_col
+    mask = jnp.concatenate([mask_ref[...].astype(F32), jnp.zeros((rows, LANES - depth), F32)], axis=1)
+    mask = jnp.concatenate([mask, jnp.zeros((LANES - rows, LANES), F32)], axis=0).T
+    mask_col = jnp.concatenate([mask[:depth, j : j + 1] for j in range(rows)], axis=0)
+    proj = dot(normed, map_ref[...], 1, 1) * mask_col
     left = proj[:, :tensor].astype(BF16)
     turned = jnp.concatenate(
         [proj, jnp.broadcast_to(mask_col, (rows * depth, LANES - 2 * tensor))], axis=1
@@ -266,11 +289,14 @@
         mask_rows = jnp.where(row_of == j, spread, mask_rows)
     mask_rows = jnp.concatenate([mask_rows, jnp.zeros((4 * rows, LANES - depth), F32)], axis=1)
     packed = jnp.concatenate(pieces + [mask_rows], axis=0).astype(BF16)
-    send_a[...] = packed
-    recv_a[me] = packed
-    pl.semaphore_wait(barrier, n - 1)
-    exchange(n, me, lambda peer: send_a, recv_a, sems.at[0], sems.at[1])
-
+    recv_a[stages[0][1]] = packed
+    pl.semaphore_wait(barrier, 7)
+    forward(0)
+
+    for t in range(2):
+        w_turned[t] = w_in_ref[t, :, : 4 * width].astype(F32).T.astype(BF16)
+    gathered(0, 1)
+    forward(1)
     wide[...] = outer_ref[...].astype(F32)
     for q in range(tensor):
         weight = wide[pl.ds(q, tensor, stride=tensor), :].astype(BF16)
@@ -280,8 +306,8 @@
             factors[place : place + depth, i * width : (i + 1) * width] = factor[
                 i * depth : (i + 1) * depth
             ]
-    for t in range(2):
-        w_turned[t] = w_in_ref[t, :, : 4 * width].astype(F32).T.astype(BF16)
+    gathered(1, 1)
+    forward(2)
     seq = seq_ref[...].astype(F32)
     lane = lax.broadcasted_iota(jnp.int32, seq.shape, 1)
     pair_mask = jnp.concatenate(
@@ -292,11 +318,13 @@
         axis=1,
     )
 
-    await_bytes(n, recv_a, sems.at[1])
+    gathered(2, 1)
     total = n * rows
     kept = rows * blocks
-    wide[...] = recv_a[:, :kept, :].astype(F32).reshape(n * kept, LANES)
-    first[...] = recv_a[:, kept:, :].astype(F32).reshape(4 * total, LANES)
+    for d in range(n):
+        slot = d % 2 * 16 + d // 2 % 4 * 4 + d // 8
+        wide[d * kept : (d + 1) * kept, :] = recv_a[slot, :kept, :].astype(F32)
+        first[d * 4 * rows : (d + 1) * 4 * rows, :] = recv_a[slot, kept:, :].astype(F32)
     right = jnp.concatenate(
         [wide[pl.ds(b, total, stride=blocks), :].astype(BF16) for b in range(blocks)], axis=1
     )
@@ -352,7 +380,8 @@
         current = following
     for r in range(rows):
         out_ref[r] = current[r]
-    await_bytes(n, recv_a, sems.at[0])
+    for stage in range(3):
+        gathered(stage, 0)
     for t in range(2):
         await_bytes(n, recv_b.at[t], sems.at[2 + 4 * t])
         await_bytes(n, recv_c.at[t], sems.at[4 + 4 * t])
@@ -384,7 +413,6 @@
         in_specs=[vmem] * 11,
         out_specs=vmem,
         scratch_shapes=[
-            pltpu.VMEM((kept + 4 * rows, LANES), BF16),
             pltpu.VMEM((n, kept + 4 * rows, LANES), BF16),
             pltpu.VMEM((2, n, 2 * strip, total), BF16),
             pltpu.VMEM((2, n, 2 * strip, total), BF16),
@@ -397,17 +425,18 @@
             pltpu.VMEM((outer, rows * width), BF16),
             pltpu.VMEM((2, 4 * width, width), BF16),
             pltpu.SemaphoreType.DMA((10,)),
+            pltpu.SemaphoreType.DMA((2, 3)),
         ],
         compiler_params=pltpu.CompilerParams(
             collective_id=0, has_side_effects=True, vmem_limit_bytes=40 * 1024 * 1024
         ),
     )(
         jnp.transpose(homolog_embedding, (1, 0, 2)).reshape(rows * depth, channels),
-        jnp.transpose(alignment_mask).reshape(rows * depth, 1),
+        jnp.transpose(alignment_mask),
         pair_activation,
         sequence_mask.reshape(1, total),
         homolog_scaling_factor.reshape(1, channels),
-        homolog_mapping_matrix,
+        jnp.transpose(homolog_mapping_matrix),
         outer_output_weight,
         outer_output_bias.reshape(1, width),
         pair_norm_gains,

time: 52.9 us -> 49.5 us (0.936)
  Pallas kernels: 46.5 us -> 43.4 us
    pallas_call x1, Pallas kernels: 46.5 us -> 43.4 us  [fused(): pl.pallas_call(functools.partial(fused_kernel, n, rows, depth), out_shape...]
    reshape x1 -> x0, local copies, waits for them, and re-layouts: 0.79 us -> none  [fused(): jnp.transpose(alignment_mask).reshape(rows * depth, 1)]
    unnamed x18 -> x21, local copies, waits for them, and re-layouts: 4.28 us -> 4.84 us
where the time goes in v3:
time: 49.5 us; the launch traced here: 49.1 us
  Pallas kernels  43.4 us (88%)
  local copies, waits for them, and re-layouts  5.73 us (12%)
    pallas_call x1, Pallas kernels, fused(): pl.pallas_call(functools.partial(fused_kernel, n, rows, depth), out_shape...  43.4 us
    unnamed x21, local copies, waits for them, and re-layouts  4.84 us

profile of v3, /device:TPU:0, one launch (start us, length us, event | category | flops | bytes accessed | tf_op | source)
XLA Modules:
  0.0 49.1 jit_solution(2570315427584959830)
XLA Ops:
  0.0 0.0 copy-start.2
  0.0 0.0 copy-start.5
  0.0 0.0 copy-start.6
  0.0 0.0 copy-start.9
  0.0 0.9 %copy.12 = bf16[4,32,256]{2,1,0:T(8,128)(2,1)S(1)} copy(bf16[4,32,256]{2,0,1:T(4,128)(2,1)} %bitcast.13) | data formatting | bytes 131072 | tf_op jit(solution)/shard_map/transpose | solution.py:434
  0.9 0.0 copy-start.7
  0.9 0.0 copy-start.8
  0.9 0.0 copy-done.2
  0.9 0.0 copy-done.5
  0.9 0.0 copy-done.6
  0.9 0.0 copy-done.9
  1.0 0.6 %copy-done.7 = f32[256]{0:T(256)S(1)} copy-done((f32[256]{0:T(256)S(1)}, f32[256]{0:T(256)}, u32[]{:S(2)}) %copy-start.7) | copy-done | bytes 1048
  1.6 0.0 copy-done.8
  1.6 0.0 copy-start
  1.6 1.0 %copy-done = bf16[2,128,640]{2,1,0:T(8,128)(2,1)S(1)} copy-done((bf16[2,128,640]{2,1,0:T(8,128)(2,1)S(1)}, bf16[2,128,640]{2,1,0:T(8,128)(2,1)}, u32[]{:S(2)}) %copy-start) | copy-done | bytes 327704
  2.6 0.0 copy-start.1
  2.6 0.9 %copy-done.1 = bf16[1024,128]{1,0:T(8,128)(2,1)S(1)} copy-done((bf16[1024,128]{1,0:T(8,128)(2,1)S(1)}, bf16[1024,128]{1,0:T(8,128)(2,1)}, u32[]{:S(2)}) %copy-start.1) | copy-done | bytes 262168
  3.5 0.0 copy-start.3
  3.5 0.8 %copy-done.3 = bf16[2,128,128]{2,1,0:T(8,128)(2,1)S(1)} copy-done((bf16[2,128,128]{2,1,0:T(8,128)(2,1)S(1)}, bf16[2,128,128]{2,1,0:T(8,128)(2,1)}, u32[]{:S(2)}) %copy-start.3) | copy-done | bytes 65560
  4.4 0.0 copy-start.4
  4.4 0.8 %copy-done.4 = bf16[256,64]{0,1:T(8,128)(2,1)S(1)} copy-done((bf16[256,64]{0,1:T(8,128)(2,1)S(1)}, bf16[256,64]{0,1:T(8,128)(2,1)}, u32[]{:S(2)}) %copy-start.4) | copy-done | bytes 32792
  5.1 43.4 %shard_map.109 = bf16[4,128,128]{2,1,0:T(8,128)(2,1)S(1)} custom-call(bf16[128,256]{1,0:T(8,128)(2,1)S(1)} %bitcast.7, s32[4,32]{1,0:T(4,128)S(1)} %bitcast.9, bf16[4,128,128]{2,1,0:T(8,128)(2,1)S(1)} %copy-done.2, s32[1,128]{1,0:T(1,128)S(1)} %bitcast.11, f32[1,256]{1,0:T(1,128)S(1)} %bitcast.10, bf16[64,256]{1,0:T(8,128)(2,1)S(1)} %bitcast.8, ...), custom_call_target="tpu_custom_call" | custom-call | tf_op jit(solution)/shard_map/pallas_call | solution.py:410
  48.5 0.7 %copy.14 = bf16[4,128,128]{2,1,0:T(8,128)(2,1)} copy(bf16[4,128,128]{2,1,0:T(8,128)(2,1)S(1)} %shard_map.109) | data formatting | bytes 262144
Async XLA Ops:
  0.0 0.9 %copy-start.2 = (bf16[4,128,128]{2,1,0:T(8,128)(2,1)S(1)}, bf16[4,128,128]{2,1,0:T(8,128)(2,1)}, u32[]{:S(2)}) copy-start(bf16[4,128,128]{2,1,0:T(8,128)(2,1)} %pair_ref.1) | copy-start | bytes 393220
  0.0 0.9 %copy-start.5 = (s32[32,4]{0,1:T(4,128)S(1)}, s32[32,4]{0,1:T(4,128)}, u32[]{:S(2)}) copy-start(s32[32,4]{0,1:T(4,128)} %param.12) | copy-start | bytes 1540
  0.0 0.9 %copy-start.6 = (f32[4,128]{1,0:T(4,128)S(1)}, f32[4,128]{1,0:T(4,128)}, u32[]{:S(2)}) copy-start(f32[4,128]{1,0:T(4,128)} %gains_ref.1) | copy-start | bytes 6148
  0.0 0.9 %copy-start.9 = (f32[128]{0:T(128)S(1)}, f32[128]{0:T(128)}, u32[]{:S(2)}) copy-start(f32[128]{0:T(128)} %param.18) | copy-start | bytes 1540
  0.9 0.7 %copy-start.7 = (f32[256]{0:T(256)S(1)}, f32[256]{0:T(256)}, u32[]{:S(2)}) copy-start(f32[256]{0:T(256)} %param.15) | copy-start | bytes 3076
  0.9 0.7 %copy-start.8 = (s32[128]{0:T(128)S(1)}, s32[128]{0:T(128)}, u32[]{:S(2)}) copy-start(s32[128]{0:T(128)} %param.14) | copy-start | bytes 1540
  1.6 1.0 %copy-start = (bf16[2,128,640]{2,1,0:T(8,128)(2,1)S(1)}, bf16[2,128,640]{2,1,0:T(8,128)(2,1)}, u32[]{:S(2)}) copy-start(bf16[2,128,640]{2,1,0:T(8,128)(2,1)} %w_in_ref.1) | copy-start | bytes 983044
  2.6 0.9 %copy-start.1 = (bf16[1024,128]{1,0:T(8,128)(2,1)S(1)}, bf16[1024,128]{1,0:T(8,128)(2,1)}, u32[]{:S(2)}) copy-start(bf16[1024,128]{1,0:T(8,128)(2,1)} %outer_ref.1) | copy-start | bytes 786436
  3.5 0.8 %copy-start.3 = (bf16[2,128,128]{2,1,0:T(8,128)(2,1)S(1)}, bf16[2,128,128]{2,1,0:T(8,128)(2,1)}, u32[]{:S(2)}) copy-start(bf16[2,128,128]{2,1,0:T(8,128)(2,1)} %w_out_ref.1) | copy-start | bytes 196612
  4.4 0.8 %copy-start.4 = (bf16[256,64]{0,1:T(8,128)(2,1)S(1)}, bf16[256,64]{0,1:T(8,128)(2,1)}, u32[]{:S(2)}) copy-start(bf16[256,64]{0,1:T(8,128)(2,1)} %param.16) | copy-start | bytes 98308

commit v4 on v3

--- a/solution.py
+++ b/solution.py
@@ -184,7 +184,7 @@
         ).start()
         return carry
 
-    lax.fori_loop(1, n, start, 0)
+    lax.fori_loop(1, n, start, 0, unroll=True)
 
 
 def await_bytes(n, arrived, sem):
@@ -198,15 +198,15 @@
     depth,
     x_ref,
     mask_ref,
-    pair_ref,
+    pair_hbm,
     seq_ref,
     scale_ref,
-    map_ref,
-    outer_ref,
+    map_hbm,
+    outer_hbm,
     bias_ref,
     gains_ref,
-    w_in_ref,
-    w_out_ref,
+    w_in_hbm,
+    w_out_hbm,
     out_ref,
     recv_a,
     send_b,
@@ -221,7 +221,27 @@
     w_turned,
     sems,
     gather_sems,
+    map_ref,
+    outer_ref,
+    w_in_ref,
+    pair_ref,
+    w_out_ref,
+    load_sems,
 ):
+    loads = [
+        pltpu.make_async_copy(far_away, near, load_sems.at[k])
+        for k, (far_away, near) in enumerate(
+            (
+                (map_hbm, map_ref),
+                (w_in_hbm, w_in_ref),
+                (outer_hbm, outer_ref),
+                (pair_hbm, pair_ref),
+                (w_out_hbm, w_out_ref),
+            )
+        )
+    ]
+    for load in loads:
+        load.start()
     me = lax.axis_index("dap")
     barrier = pltpu.get_barrier_semaphore()
 
@@ -265,6 +285,7 @@
     mask = jnp.concatenate([mask_ref[...].astype(F32), jnp.zeros((rows, LANES - depth), F32)], axis=1)
     mask = jnp.concatenate([mask, jnp.zeros((LANES - rows, LANES), F32)], axis=0).T
     mask_col = jnp.concatenate([mask[:depth, j : j + 1] for j in range(rows)], axis=0)
+    loads[0].wait()
     proj = dot(normed, map_ref[...], 1, 1) * mask_col
     left = proj[:, :tensor].astype(BF16)
     turned = jnp.concatenate(
@@ -293,10 +314,12 @@
     pl.semaphore_wait(barrier, 7)
     forward(0)
 
+    loads[1].wait()
     for t in range(2):
         w_turned[t] = w_in_ref[t, :, : 4 * width].astype(F32).T.astype(BF16)
     gathered(0, 1)
     forward(1)
+    loads[2].wait()
     wide[...] = outer_ref[...].astype(F32)
     for q in range(tensor):
         weight = wide[pl.ds(q, tensor, stride=tensor), :].astype(BF16)
@@ -308,6 +331,8 @@
             ]
     gathered(1, 1)
     forward(2)
+    loads[3].wait()
+    loads[4].wait()
     seq = seq_ref[...].astype(F32)
     lane = lax.broadcasted_iota(jnp.int32, seq.shape, 1)
     pair_mask = jnp.concatenate(
@@ -347,26 +372,31 @@
             gated = pair_mask * jax.nn.sigmoid(gate) * value
             for r in range(rows):
                 scratch[r * width : (r + 1) * width, :] = gated[:, r * total : (r + 1) * total]
-        for d in range(n):
-            send_b[t, d, :strip, :] = first[pl.ds(d, strip, stride=n), :].astype(BF16)
-            send_b[t, d, strip:, :] = second[pl.ds(d, strip, stride=n), :].astype(BF16)
-        s = 2 + 4 * t
-        exchange(n, me, lambda peer: send_b.at[t, peer], recv_b.at[t], sems.at[s], sems.at[s + 1])
-        recv_b[t, me] = send_b[t, me]
+            for d in range(n):
+                send_b[t, side, d] = scratch[pl.ds(d, strip, stride=n), :].astype(BF16)
+            exchange(
+                n,
+                me,
+                lambda peer: send_b.at[t, side, peer],
+                recv_b.at[t, side],
+                sems.at[t, side, 0],
+                sems.at[t, side, 1],
+            )
+            recv_b[t, side, me] = send_b[t, side, me]
         gating = jax.nn.sigmoid(dot(normed, w_in_ref[t, :, 4 * width :], 1, 0))
         gain = jnp.broadcast_to(gains_ref[2 * t + 1 : 2 * t + 2, :], (total, width)).T
-        await_bytes(n, recv_b.at[t], sems.at[s + 1])
-        first[...] = recv_b[t, :, :strip, :].astype(F32).reshape(n * strip, LANES)
-        second[...] = recv_b[t, :, strip:, :].astype(F32).reshape(n * strip, LANES)
+        for side, scratch in ((0, first), (1, second)):
+            await_bytes(n, recv_b.at[t, side], sems.at[t, side, 1])
+            scratch[...] = recv_b[t, side].astype(F32).reshape(n * strip, LANES)
         for c in range(per):
             one = first[pl.ds(c, total, stride=per), :].astype(BF16)
             two = second[pl.ds(c, total, stride=per), :].astype(BF16)
             over = 1 - t
             mixed_rows[pl.ds(c, total, stride=per), :] = dot(one, two, over, over)
         send_c[t] = mixed_rows[...].astype(BF16).reshape(n, strip, LANES)
-        exchange(n, me, lambda peer: send_c.at[t, peer], recv_c.at[t], sems.at[s + 2], sems.at[s + 3])
+        exchange(n, me, lambda peer: send_c.at[t, peer], recv_c.at[t], sems.at[t, 2, 0], sems.at[t, 2, 1])
         recv_c[t, me] = send_c[t, me]
-        await_bytes(n, recv_c.at[t], sems.at[s + 3])
+        await_bytes(n, recv_c.at[t], sems.at[t, 2, 1])
         first[...] = recv_c[t].astype(F32).reshape(n * strip, LANES)
         following = []
         for r in range(rows):
@@ -383,8 +413,9 @@
     for stage in range(3):
         gathered(stage, 0)
     for t in range(2):
-        await_bytes(n, recv_b.at[t], sems.at[2 + 4 * t])
-        await_bytes(n, recv_c.at[t], sems.at[4 + 4 * t])
+        for side in range(2):
+            await_bytes(n, recv_b.at[t, side], sems.at[t, side, 0])
+        await_bytes(n, recv_c.at[t], sems.at[t, 2, 0])
 
 
 def fused(
@@ -407,15 +438,16 @@
     outer = outer_output_weight.shape[0]
     kept = rows * (homolog_mapping_matrix.shape[1] // 2) * depth // LANES
     vmem = pl.BlockSpec(memory_space=pltpu.VMEM)
+    hbm = pl.BlockSpec(memory_space=pltpu.HBM)
     return pl.pallas_call(
         functools.partial(fused_kernel, n, rows, depth),
         out_shape=jax.ShapeDtypeStruct(pair_activation.shape, BF16),
-        in_specs=[vmem] * 11,
+        in_specs=[vmem, vmem, hbm, vmem, vmem, hbm, hbm, vmem, vmem, hbm, hbm],
         out_specs=vmem,
         scratch_shapes=[
             pltpu.VMEM((n, kept + 4 * rows, LANES), BF16),
-            pltpu.VMEM((2, n, 2 * strip, total), BF16),
-            pltpu.VMEM((2, n, 2 * strip, total), BF16),
+            pltpu.VMEM((2, 2, n, strip, total), BF16),
+            pltpu.VMEM((2, 2, n, strip, total), BF16),
             pltpu.VMEM((2, n, strip, total), BF16),
             pltpu.VMEM((2, n, strip, total), BF16),
             pltpu.VMEM((outer, width), F32),
@@ -424,11 +456,17 @@
             pltpu.VMEM((rows * width, LANES), F32),
             pltpu.VMEM((outer, rows * width), BF16),
             pltpu.VMEM((2, 4 * width, width), BF16),
-            pltpu.SemaphoreType.DMA((10,)),
+            pltpu.SemaphoreType.DMA((2, 3, 2)),
             pltpu.SemaphoreType.DMA((2, 3)),
+            pltpu.VMEM(homolog_mapping_matrix.shape[::-1], BF16),
+            pltpu.VMEM(outer_output_weight.shape, BF16),
+            pltpu.VMEM(triangle_input_weights.shape, BF16),
+            pltpu.VMEM(pair_activation.shape, BF16),
+            pltpu.VMEM(triangle_output_weights.shape, BF16),
+            pltpu.SemaphoreType.DMA((5,)),
         ],
         compiler_params=pltpu.CompilerParams(
-            collective_id=0, has_side_effects=True, vmem_limit_bytes=40 * 1024 * 1024
+            collective_id=0, has_side_effects=True, vmem_limit_bytes=62 * 1024 * 1024
         ),
     )(
         jnp.transpose(homolog_embedding, (1, 0, 2)).reshape(rows * depth, channels),

time: 49.5 us -> 47.7 us (0.964)
  local copies, waits for them, and re-layouts: 5.73 us -> 3.05 us
  Pallas kernels: 43.4 us -> 44.4 us
    unnamed x21 -> x1, local copies, waits for them, and re-layouts: 4.84 us -> 1.57 us
    pallas_call x1, Pallas kernels: 43.4 us -> 44.4 us  [fused(): pl.pallas_call(functools.partial(fused_kernel, n, rows, depth), out_shape...]
    transpose x1, local copies, waits for them, and re-layouts: 0.88 us -> 1.48 us  [fused(): jnp.transpose(homolog_embedding, (1, 0, 2)).reshape(rows * depth, channels)]
where the time goes in v4:
time: 47.7 us; the launch traced here: 47.5 us
  Pallas kernels  44.4 us (93%)
  local copies, waits for them, and re-layouts  3.05 us (6%)
    pallas_call x1, Pallas kernels, fused(): pl.pallas_call(functools.partial(fused_kernel, n, rows, depth), out_shape...  44.4 us
    unnamed x1, local copies, waits for them, and re-layouts  1.57 us
    transpose x1, local copies, waits for them, and re-layouts, fused(): jnp.transpose(homolog_embedding, (1, 0, 2)).reshape(rows * depth, channels)  1.48 us

profile of v4, /device:TPU:0, one launch (start us, length us, event | category | flops | bytes accessed | tf_op | source)
XLA Modules:
  0.0 47.5 jit_solution(5643559310866122708)
XLA Ops:
  0.0 1.5 %copy.12 = bf16[4,32,256]{2,1,0:T(8,128)(2,1)} copy(bf16[4,32,256]{2,0,1:T(4,128)(2,1)} %bitcast.8) | data formatting | bytes 131072 | tf_op jit(solution)/shard_map/transpose | solution.py:472
  1.5 44.4 %shard_map.109 = bf16[4,128,128]{2,1,0:T(8,128)(2,1)} custom-call(bf16[128,256]{1,0:T(8,128)(2,1)} %bitcast.7, s32[4,32]{1,0:T(4,128)} %bitcast.10, bf16[4,128,128]{2,1,0:T(8,128)(2,1)} %pair_hbm.1, s32[1,128]{1,0:T(1,128)} %bitcast.12, f32[1,256]{1,0:T(1,128)} %bitcast.11, bf16[64,256]{1,0:T(8,128)(2,1)} %bitcast.9, bf16[1024,128]{1,0:T(8,128)(2,1)} %outer_hbm.1, ...), custom_call_target="tpu_custom_call" | custom-call | tf_op jit(solution)/shard_map/pallas_call | solution.py:442
  45.9 1.6 %copy.14 = bf16[4,128,128]{2,1,0:T(8,128)(2,1)} copy(bf16[4,128,128]{2,1,0:T(8,128)(2,1)} %shard_map.109) | data formatting | bytes 262144

commit v5 on v4

--- a/solution.py
+++ b/solution.py
@@ -249,30 +249,26 @@
     far_peers = [lax.rem(me + 8 * p, n) for p in range(1, 4)]
     chip_peers = [far * 8 + lax.rem(chip + p, 4) * 2 + core for p in range(1, 4)]
     core_peers = [me + 1 - 2 * core]
-    stages = (
-        (far_peers, core * 16 + chip * 4 + far, 1),
-        (chip_peers, core * 16 + chip * 4, 4),
-        (core_peers, core * 16, 16),
-    )
+    column = core * 16 + chip * 4
+    own_slot = column + far
     for peer in far_peers + chip_peers + core_peers:
         pl.semaphore_signal(barrier, inc=1, device_id={"dap": peer}, device_id_type=MESH)
 
-    def forward(stage):
-        peers, slot, count = stages[stage]
+    def forward(peers, slot, count, send, arrivals):
         held = recv_a.at[pl.ds(slot, count)]
-        for peer in peers:
+        for peer, arrival in zip(peers, arrivals):
             pltpu.make_async_remote_copy(
                 src_ref=held,
                 dst_ref=held,
-                send_sem=gather_sems.at[0, stage],
-                recv_sem=gather_sems.at[1, stage],
+                send_sem=gather_sems.at[send],
+                recv_sem=gather_sems.at[arrival],
                 device_id={"dap": peer},
                 device_id_type=MESH,
             ).start()
 
-    def gathered(stage, way):
-        blocks_moved = recv_a.at[pl.ds(0, len(stages[stage][0]) * stages[stage][2])]
-        pltpu.make_async_copy(blocks_moved, blocks_moved, gather_sems.at[way, stage]).wait()
+    def gathered(count, sem):
+        blocks_moved = recv_a.at[pl.ds(0, count)]
+        pltpu.make_async_copy(blocks_moved, blocks_moved, gather_sems.at[sem]).wait()
 
     width = pair_ref.shape[2]
     tensor = map_ref.shape[0] // 2
@@ -310,15 +306,15 @@
         mask_rows = jnp.where(row_of == j, spread, mask_rows)
     mask_rows = jnp.concatenate([mask_rows, jnp.zeros((4 * rows, LANES - depth), F32)], axis=1)
     packed = jnp.concatenate(pieces + [mask_rows], axis=0).astype(BF16)
-    recv_a[stages[0][1]] = packed
+    recv_a[own_slot] = packed
     pl.semaphore_wait(barrier, 7)
-    forward(0)
-
-    loads[1].wait()
-    for t in range(2):
-        w_turned[t] = w_in_ref[t, :, : 4 * width].astype(F32).T.astype(BF16)
-    gathered(0, 1)
-    forward(1)
+    forward(far_peers, own_slot, 1, 0, (3, 4, 5))
+    forward(chip_peers, own_slot, 1, 1, (6, 7, 8))
+
+    for p in range(1, 4):
+        gathered(1, 2 + p)
+        forward(chip_peers, column + lax.rem(far + 4 - p, 4), 1, 1, (6, 7, 8))
+    forward(core_peers, column, 4, 2, (9,))
     loads[2].wait()
     wide[...] = outer_ref[...].astype(F32)
     for q in range(tensor):
@@ -329,8 +325,12 @@
             factors[place : place + depth, i * width : (i + 1) * width] = factor[
                 i * depth : (i + 1) * depth
             ]
-    gathered(1, 1)
-    forward(2)
+    for p in range(1, 4):
+        gathered(4, 5 + p)
+        forward(core_peers, core * 16 + lax.rem(chip + 4 - p, 4) * 4, 4, 2, (9,))
+    loads[1].wait()
+    for t in range(2):
+        w_turned[t] = w_in_ref[t, :, : 4 * width].astype(F32).T.astype(BF16)
     loads[3].wait()
     loads[4].wait()
     seq = seq_ref[...].astype(F32)
@@ -343,7 +343,7 @@
         axis=1,
     )
 
-    gathered(2, 1)
+    gathered(16, 9)
     total = n * rows
     kept = rows * blocks
     for d in range(n):
@@ -410,8 +410,8 @@
         current = following
     for r in range(rows):
         out_ref[r] = current[r]
-    for stage in range(3):
-        gathered(stage, 0)
+    for stage, count in enumerate((3, 12, 16)):
+        gathered(count, stage)
     for t in range(2):
         for side in range(2):
             await_bytes(n, recv_b.at[t, side], sems.at[t, side, 0])
@@ -457,7 +457,7 @@
             pltpu.VMEM((outer, rows * width), BF16),
             pltpu.VMEM((2, 4 * width, width), BF16),
             pltpu.SemaphoreType.DMA((2, 3, 2)),
-            pltpu.SemaphoreType.DMA((2, 3)),
+            pltpu.SemaphoreType.DMA((10,)),
             pltpu.VMEM(homolog_mapping_matrix.shape[::-1], BF16),
             pltpu.VMEM(outer_output_weight.shape, BF16),
             pltpu.VMEM(triangle_input_weights.shape, BF16),

time: 47.7 us -> 48 us (level)
  no operation moved by 1% of the time
where the time goes in v5:
time: 48 us; the launch traced here: 47.8 us
  Pallas kernels  44.7 us (93%)
  local copies, waits for them, and re-layouts  3.05 us (6%)
    pallas_call x1, Pallas kernels, fused(): pl.pallas_call(functools.partial(fused_kernel, n, rows, depth), out_shape...  44.7 us
    unnamed x1, local copies, waits for them, and re-layouts  1.57 us
    transpose x1, local copies, waits for them, and re-layouts, fused(): jnp.transpose(homolog_embedding, (1, 0, 2)).reshape(rows * depth, channels)  1.48 us

profile of v5, /device:TPU:0, one launch (start us, length us, event | category | flops | bytes accessed | tf_op | source)
XLA Modules:
  0.0 47.8 jit_solution(17328986821615484928)
XLA Ops:
  0.0 1.5 %copy.12 = bf16[4,32,256]{2,1,0:T(8,128)(2,1)} copy(bf16[4,32,256]{2,0,1:T(4,128)(2,1)} %bitcast.8) | data formatting | bytes 131072 | tf_op jit(solution)/shard_map/transpose | solution.py:472
  1.5 44.7 %shard_map.109 = bf16[4,128,128]{2,1,0:T(8,128)(2,1)} custom-call(bf16[128,256]{1,0:T(8,128)(2,1)} %bitcast.7, s32[4,32]{1,0:T(4,128)} %bitcast.10, bf16[4,128,128]{2,1,0:T(8,128)(2,1)} %pair_hbm.1, s32[1,128]{1,0:T(1,128)} %bitcast.12, f32[1,256]{1,0:T(1,128)} %bitcast.11, bf16[64,256]{1,0:T(8,128)(2,1)} %bitcast.9, bf16[1024,128]{1,0:T(8,128)(2,1)} %outer_hbm.1, ...), custom_call_target="tpu_custom_call" | custom-call | tf_op jit(solution)/shard_map/pallas_call | solution.py:442
  46.2 1.6 %copy.14 = bf16[4,128,128]{2,1,0:T(8,128)(2,1)} copy(bf16[4,128,128]{2,1,0:T(8,128)(2,1)} %shard_map.109) | data formatting | bytes 262144

commit v6 on v4

--- a/solution.py
+++ b/solution.py
@@ -373,21 +373,17 @@
             for r in range(rows):
                 scratch[r * width : (r + 1) * width, :] = gated[:, r * total : (r + 1) * total]
             for d in range(n):
-                send_b[t, side, d] = scratch[pl.ds(d, strip, stride=n), :].astype(BF16)
-            exchange(
-                n,
-                me,
-                lambda peer: send_b.at[t, side, peer],
-                recv_b.at[t, side],
-                sems.at[t, side, 0],
-                sems.at[t, side, 1],
-            )
-            recv_b[t, side, me] = send_b[t, side, me]
+                part = slice(side * strip, (side + 1) * strip)
+                send_b[t, d, part, :] = scratch[pl.ds(d, strip, stride=n), :].astype(BF16)
+        exchange(
+            n, me, lambda peer: send_b.at[t, peer], recv_b.at[t], sems.at[t, 0, 0], sems.at[t, 0, 1]
+        )
+        recv_b[t, me] = send_b[t, me]
         gating = jax.nn.sigmoid(dot(normed, w_in_ref[t, :, 4 * width :], 1, 0))
         gain = jnp.broadcast_to(gains_ref[2 * t + 1 : 2 * t + 2, :], (total, width)).T
-        for side, scratch in ((0, first), (1, second)):
-            await_bytes(n, recv_b.at[t, side], sems.at[t, side, 1])
-            scratch[...] = recv_b[t, side].astype(F32).reshape(n * strip, LANES)
+        await_bytes(n, recv_b.at[t], sems.at[t, 0, 1])
+        first[...] = recv_b[t, :, :strip, :].astype(F32).reshape(n * strip, LANES)
+        second[...] = recv_b[t, :, strip:, :].astype(F32).reshape(n * strip, LANES)
         for c in range(per):
             one = first[pl.ds(c, total, stride=per), :].astype(BF16)
             two = second[pl.ds(c, total, stride=per), :].astype(BF16)
@@ -413,8 +409,7 @@
     for stage in range(3):
         gathered(stage, 0)
     for t in range(2):
-        for side in range(2):
-            await_bytes(n, recv_b.at[t, side], sems.at[t, side, 0])
+        await_bytes(n, recv_b.at[t], sems.at[t, 0, 0])
         await_bytes(n, recv_c.at[t], sems.at[t, 2, 0])
 
 
@@ -446,8 +441,8 @@
         out_specs=vmem,
         scratch_shapes=[
             pltpu.VMEM((n, kept + 4 * rows, LANES), BF16),
-            pltpu.VMEM((2, 2, n, strip, total), BF16),
-            pltpu.VMEM((2, 2, n, strip, total), BF16),
+            pltpu.VMEM((2, n, 2 * strip, total), BF16),
+            pltpu.VMEM((2, n, 2 * strip, total), BF16),
             pltpu.VMEM((2, n, strip, total), BF16),
             pltpu.VMEM((2, n, strip, total), BF16),
             pltpu.VMEM((outer, width), F32),

time: 47.7 us -> 48 us (level)
  no operation moved by 1% of the time
where the time goes in v6:
time: 48 us; the launch traced here: 47.8 us
  Pallas kernels  44.7 us (93%)
  local copies, waits for them, and re-layouts  3.05 us (6%)
    pallas_call x1, Pallas kernels, fused(): pl.pallas_call(functools.partial(fused_kernel, n, rows, depth), out_shape...  44.7 us
    unnamed x1, local copies, waits for them, and re-layouts  1.57 us
    transpose x1, local copies, waits for them, and re-layouts, fused(): jnp.transpose(homolog_embedding, (1, 0, 2)).reshape(rows * depth, channels)  1.48 us

profile of v6, /device:TPU:0, one launch (start us, length us, event | category | flops | bytes accessed | tf_op | source)
XLA Modules:
  0.0 47.8 jit_solution(17625646958719627279)
XLA Ops:
  0.0 1.5 %copy.12 = bf16[4,32,256]{2,1,0:T(8,128)(2,1)} copy(bf16[4,32,256]{2,0,1:T(4,128)(2,1)} %bitcast.8) | data formatting | bytes 131072 | tf_op jit(solution)/shard_map/transpose | solution.py:467
  1.5 44.7 %shard_map.109 = bf16[4,128,128]{2,1,0:T(8,128)(2,1)} custom-call(bf16[128,256]{1,0:T(8,128)(2,1)} %bitcast.7, s32[4,32]{1,0:T(4,128)} %bitcast.10, bf16[4,128,128]{2,1,0:T(8,128)(2,1)} %pair_hbm.1, s32[1,128]{1,0:T(1,128)} %bitcast.12, f32[1,256]{1,0:T(1,128)} %bitcast.11, bf16[64,256]{1,0:T(8,128)(2,1)} %bitcast.9, bf16[1024,128]{1,0:T(8,128)(2,1)} %outer_hbm.1, ...), custom_call_target="tpu_custom_call" | custom-call | tf_op jit(solution)/shard_map/pallas_call | solution.py:437
  46.2 1.6 %copy.14 = bf16[4,128,128]{2,1,0:T(8,128)(2,1)} copy(bf16[4,128,128]{2,1,0:T(8,128)(2,1)} %shard_map.109) | data formatting | bytes 262144
